TPU v7x, 128 devices: a whole 4x4x4 slice. The times are simulated.
128 devices in a mesh: ctx: 8 (over y_lo, x), exp: 16 (over z, y_hi, core).
Axes of the slice: x: 4, y: 4 (y_hi: 2, y_lo: 2; y = y_hi * 2 + y_lo), z: 4, core: 2. Of those that a mesh axis runs over, the one named last changes fastest.
Arguments:
- resid_in: bfloat16 [16384, 2880], P(('exp', 'ctx')), may hold values from -6 to 6
- queries: bfloat16 [16384, 4096], P(('exp', 'ctx')), may hold values from -6 to 6
- keys: bfloat16 [16384, 512], P(('exp', 'ctx')), may hold values from -6 to 6
- values: bfloat16 [16384, 512], P(('exp', 'ctx')), may hold values from -6 to 6
- sinks: float32 [64], replicated, may hold values from 2 to 7
- segments: int32 [16384], P(('exp', 'ctx')), may hold values from 0 to 31, never falling along the last dimension, each value on 1 to 1024 neighbouring positions
- norm_gain: float32 [2880], replicated, may hold values from 0.1 to 1.9
- out_weight: bfloat16 [4096, 2880], P('ctx'), may hold values from -0.75 to 0.75
- gate_weight: bfloat16 [16, 2880, 2880], P('exp', None, 'ctx'), may hold values from -0.109375 to 0.109375
- up_weight: bfloat16 [16, 2880, 2880], P('exp', None, 'ctx'), may hold values from -0.109375 to 0.109375
- down_weight: bfloat16 [16, 2880, 2880], P('exp', 'ctx'), may hold values from -0.109375 to 0.109375
- expert_ids: int32 [16384, 4], P(('exp', 'ctx')), may hold values from 0 to 127, as said below
- route_weights: float32 [16384, 4], P(('exp', 'ctx')), may hold values from 0.1 to 1
Outputs:
- resid_out: bfloat16 [16384, 2880], P(('exp', 'ctx'))
Inputs may be any that keep to these rules, and one draw needn't show every extreme that they name: `expert_ids`: column k of a row names an expert in [k * 32, (k + 1) * 32). Within the rows of one device (aligned blocks of 128 rows) no evaluated expert is named more than 8 times, and one evaluated expert is named exactly 8 times in every block.
All inputs are finite; a program needn't handle non-finite values.
Results may differ from a plain program's by a relative error of at most 0.018.
Values may be sent and summed in bfloat16 or wider, within the bound.
No kernel may reach another device: no remote copies, remote signals or barrier semaphores. Data moves between devices by JAX's collectives and lax.ppermute only.
A program may use at most 128 MiB of HBM per device.

v0:
```python
import jax
import jax.numpy as jnp
from jax import lax
from jax.sharding import PartitionSpec as P

D = 2880
QUERY_HEADS = 64
KEY_VALUE_HEADS = 8
HEAD_SIZE = 64
ALL_EXPERTS = 128
TOPK = 4
CAP = 8


def expert_act(rows_x, gate_here, up_here):
    gate = jnp.dot(rows_x, gate_here, preferred_element_type=jnp.float32)
    upper = jnp.dot(rows_x, up_here, preferred_element_type=jnp.float32)
    return ((upper + 1.0) * gate * jax.nn.sigmoid(1.702 * gate)).astype(jnp.bfloat16)


def on_device(
    resid_in,
    queries,
    keys,
    values,
    sinks,
    segments,
    norm_gain,
    out_weight,
    gate_weight,
    up_weight,
    down_weight,
    expert_ids,
    route_weights,
):
    n_ctx = lax.axis_size("ctx")
    n_exp = lax.axis_size("exp")
    token_rows = queries.shape[0]
    query_group = QUERY_HEADS // KEY_VALUE_HEADS
    my_start = lax.axis_index("ctx") * token_rows
    query_layout = queries.reshape(token_rows, KEY_VALUE_HEADS, query_group, HEAD_SIZE)
    query_places = my_start + jnp.arange(token_rows)
    sink_layout = sinks.reshape(1, KEY_VALUE_HEADS, query_group)
    doc_wire = segments.astype(jnp.bfloat16)
    key_section = lax.all_gather(keys, "ctx", axis=0, tiled=True)
    value_section = lax.all_gather(values, "ctx", axis=0, tiled=True)
    doc_piece = lax.all_gather(doc_wire, "ctx", axis=0, tiled=True)
    entry_count = key_section.shape[0]
    key_docs = doc_piece.astype(jnp.int32)
    top_choice = jnp.broadcast_to(sink_layout, (token_rows, KEY_VALUE_HEADS, query_group))
    softmax_divisor = jnp.ones((token_rows, KEY_VALUE_HEADS, query_group), jnp.float32)
    running_total = jnp.zeros((token_rows, KEY_VALUE_HEADS, query_group, HEAD_SIZE), jnp.float32)
    scores = (
        jnp.einsum(
            "rgjd,kgd->rgjk",
            query_layout,
            key_section.reshape(entry_count, KEY_VALUE_HEADS, HEAD_SIZE),
            preferred_element_type=jnp.float32,
        )
        * 0.125
    )
    key_places = jnp.arange(entry_count)
    allowed = (key_places[None, :] <= query_places[:, None]) & (
        key_docs[None, :] == segments[:, None]
    )
    scores = jnp.where(allowed[:, None, None, :], scores, -jnp.inf)
    new_top = jnp.maximum(top_choice, jnp.max(scores, axis=-1))
    prob = jnp.exp(scores - new_top[..., None])
    shrink = jnp.exp(top_choice - new_top)
    softmax_divisor = softmax_divisor * shrink + jnp.sum(prob, axis=-1)
    running_total = running_total * shrink[..., None] + jnp.einsum(
        "rgjk,kgd->rgjd",
        prob.astype(jnp.bfloat16),
        value_section.reshape(entry_count, KEY_VALUE_HEADS, HEAD_SIZE),
        preferred_element_type=jnp.float32,
    )
    top_choice, softmax_divisor, running_total = (new_top, softmax_divisor, running_total)
    attn = (
        (running_total / softmax_divisor[..., None])
        .reshape(token_rows, QUERY_HEADS * HEAD_SIZE)
        .astype(jnp.bfloat16)
    )
    head_rows = lax.all_to_all(attn, "ctx", split_axis=1, concat_axis=0, tiled=True)
    proj = lax.psum_scatter(
        jnp.dot(head_rows, out_weight, preferred_element_type=jnp.float32).astype(jnp.bfloat16),
        "ctx",
        scatter_dimension=0,
        tiled=True,
    ).astype(jnp.float32)
    hidden = resid_in.astype(jnp.float32) + proj
    scale = lax.rsqrt(jnp.mean(hidden * hidden, axis=-1, keepdims=True) + 1e-05)
    normed = (hidden * scale * norm_gain[None, :]).astype(jnp.bfloat16)
    quarter = ALL_EXPERTS // TOPK
    window = n_exp // TOPK
    local = expert_ids % quarter
    valid = local < window
    chosen = expert_ids // quarter * window + local
    onehot = (
        ((chosen[..., None] == jnp.arange(n_exp)) & valid[..., None])
        .astype(jnp.int32)
        .reshape(token_rows * TOPK, n_exp)
    )
    before = jnp.cumsum(onehot, axis=0) - onehot
    own_rank = jnp.sum(onehot * before, axis=-1).reshape(token_rows, TOPK)
    slots_total = n_exp * CAP
    slot = jnp.where(valid, chosen * CAP + own_rank, slots_total)
    token_index = jnp.broadcast_to(
        jnp.arange(token_rows, dtype=jnp.int32)[:, None], (token_rows, TOPK)
    )
    slot_token = (
        jnp.zeros((slots_total + 1,), jnp.int32)
        .at[slot.reshape(-1)]
        .set(token_index.reshape(-1))[:slots_total]
    )
    slot_live = jnp.zeros((slots_total + 1,), jnp.int32).at[slot.reshape(-1)].set(1)[:slots_total]
    send = jnp.where(slot_live[:, None] > 0, normed[slot_token], jnp.zeros((1, D), jnp.bfloat16))
    gate_here = gate_weight[0]
    up_here = up_weight[0]
    down_here = down_weight[0]
    copies = jnp.tile(send, (n_ctx, 1))
    arrived = lax.all_to_all(copies, ("ctx", "exp"), split_axis=0, concat_axis=0, tiled=True)
    act = expert_act(arrived, gate_here, up_here)
    partial_value = jnp.dot(act, down_here, preferred_element_type=jnp.float32).astype(jnp.bfloat16)
    returned = lax.all_to_all(
        partial_value, ("ctx", "exp"), split_axis=0, concat_axis=0, tiled=True
    )
    expert_out = jnp.sum(
        returned.reshape(n_ctx, slots_total, D).astype(jnp.float32), axis=0
    ).astype(jnp.bfloat16)
    safe_slot = jnp.where(valid, slot, 0)
    picked = expert_out[safe_slot].astype(jnp.float32)
    weight = jnp.where(valid, route_weights, 0.0)
    moe = jnp.sum(picked * weight[..., None], axis=1)
    return (hidden + moe).astype(jnp.bfloat16)


def solution(mesh):
    placed = (
        P(("exp", "ctx"), None),
        P(("exp", "ctx"), None),
        P(("exp", "ctx"), None),
        P(("exp", "ctx"), None),
        P(),
        P(("exp", "ctx")),
        P(),
        P("ctx", None),
        P("exp", None, "ctx"),
        P("exp", None, "ctx"),
        P("exp", "ctx", None),
        P(("exp", "ctx"), None),
        P(("exp", "ctx"), None),
    )
    return jax.shard_map(
        on_device, mesh=mesh, in_specs=placed, out_specs=P(("exp", "ctx"), None), check_vma=False
    )
```

profile of v0, /device:TPU:1, one launch (start us, length us, event | category | flops | bytes accessed | tf_op | source)
XLA Modules:
  0.0 433.8 jit_solution(248537972854181642)
XLA Ops:
  6.5 0.7 all-gather.4.cloned.1.call-update
  7.3 0.0 all-gather.6.cloned.1.call-start
  7.3 0.7 all-gather.6.cloned.1.call-update
  8.0 0.0 reduce-scatter.4.cloned.1.call-start
  8.1 0.7 convert_bitcast_fusion
  8.7 15.8 %all-gather = bf16[8,1,128]{2,1,0:T(2,128)(2,1)S(1)} all-gather(bf16[1,1,128]{2,1,0:T(2,128)(2,1)S(1)} %convert_bitcast_fusion), channel_id=1, replica_groups=mesh['ctx'=8,'exp'=16] {'ctx'}, dimensions={0}, use_global_device_ids=true | all-gather | bytes 2304 | tf_op jit(solution)/shard_map/all_gather | solution.py:47
  24.5 2.3 copy.55
  26.8 0.7 broadcast_in_dim.50
  27.5 0.9 fusion.21
  28.4 17.7 %all-gather.4.cloned.1.call-done = bf16[1024,512]{1,0:T(8,128)(2,1)} async-done(((bf16[128,512]{1,0:T(8,128)(2,1)}), bf16[1024,512]{1,0:T(8,128)(2,1)}) %all-gather.4.cloned.1.call-update) | async-done | bytes 1048592 | tf_op jit(solution)/shard_map/all_gather | solution.py:45
  46.1 2.3 copy.54
  48.3 14.6 %fusion.2 = (f32[128,8,8]{0,2,1:T(8,128)S(1)}, f32[8,1024,128,8]{2,1,3,0:T(8,128)}) fusion(pred[128,1024]{0,1:T(8,128)(4,1)S(1)} %fusion.21, bf16[1024,8,64,1]{0,2,3,1:T(8,128)(2,1)} %bitcast.88, bf16[128,8,8,64]{0,3,2,1:T(8,128)(2,1)} %bitcast.87), kind=kOutput, calls=%fused_computation.8 | convolution fusion | flops 1098899456 | bytes 35815424 | tf_op jit(solution)/shard_map/rgjd,kgd->rgjk/dot_general | solution.py:54
  62.9 0.1 broadcast_maximum_fusion
  63.0 14.3 %fusion = f32[128,8,8]{0,2,1:T(8,128)S(1)} fusion(f32[8,1024,128,8]{2,1,3,0:T(8,128)} %get-tuple-element.12, f32[128,8,8]{0,2,1:T(8,128)S(1)} %broadcast_maximum_fusion, pred[128,1024]{0,1:T(8,128)(4,1)S(1)} %fusion.21), kind=kLoop, calls=%fused_computation.6 | loop fusion | flops 33546240 | bytes 33751040 | tf_op jit(solution)/shard_map/reduce_sum | solution.py:70
  77.3 0.1 fusion.34
  77.4 8.3 %all-gather.6.cloned.1.call-done = bf16[1024,512]{1,0:T(8,128)(2,1)} async-done(((bf16[128,512]{1,0:T(8,128)(2,1)}), bf16[1024,512]{1,0:T(8,128)(2,1)}) %all-gather.6.cloned.1.call-update) | async-done | bytes 1048592 | tf_op jit(solution)/shard_map/all_gather | solution.py:46
  85.7 2.3 copy.56
  88.0 15.4 %fusion.14 = bf16[128,8,8,64]{0,3,2,1:T(8,128)(2,1)} fusion(bf16[1024,8,64,1]{0,2,3,1:T(8,128)(2,1)} %bitcast.89, f32[8,1024,128,8]{2,1,3,0:T(8,128)} %get-tuple-element.12, f32[128,8,8]{0,2,1:T(8,128)S(1)} %broadcast_maximum_fusion, pred[128,1024]{0,1:T(8,128)(4,1)S(1)} %fusion.21, f32[128,8,8]{0,2,1:T(8,128)S(1)} %get-tuple-element.10, ...), kind=kOutput, calls=%fused_computation.24 | convolution fusion | flops 1108869120 | bytes 35880960 | tf_op jit(solution)/shard_map/rgjk,kgd->rgjd/dot_general | solution.py:71
  103.3 2.3 copy.58
  105.6 14.2 %all_to_all.37 = bf16[128,8,512]{2,0,1:T(8,128)(2,1)S(1)} all-to-all(bf16[128,8,512]{2,0,1:T(8,128)(2,1)} %copy.58), channel_id=1, replica_groups=mesh['ctx'=8,'exp'=16] {'ctx'}, dimensions={1} | all-to-all | bytes 2097152 | tf_op jit(solution)/shard_map/all_to_all | solution.py:83
  119.8 5.1 %convolution_convert_fusion = bf16[1024,2880]{0,1:T(8,128)(2,1)} fusion(bf16[1024,512]{1,0:T(8,128)(2,1)S(1)} %bitcast.91, bf16[512,2880]{0,1:T(8,128)(2,1)S(1)} %copy-done), kind=kOutput, calls=%fused_computation.17 | convolution fusion | flops 3022848000 | bytes 9895936 | tf_op jit(solution)/shard_map/dot_general | solution.py:85
  124.9 8.5 %copy.74 = bf16[1024,2880]{1,0:T(8,128)(2,1)} copy(bf16[1024,2880]{0,1:T(8,128)(2,1)} %convolution_convert_fusion) | data formatting | bytes 11796480
  133.4 0.0 reduce-scatter.4.cloned.1.call-update
  133.4 0.7 copy-done.5
  134.1 0.1 copy.60
  134.2 0.1 copy.63
  134.3 0.1 copy.69
  134.5 0.1 and.43
  134.6 0.1 and.40
  134.7 0.1 fusion.23
  134.8 0.1 eq.52
  134.9 0.1 eq.48
  135.0 1.2 reduce-window.6
  136.2 0.2 slice_reduce_fusion
  136.5 0.1 fusion.29
  136.6 0.1 reshape.182
  136.7 0.1 reshape.183
  136.8 0.1 reshape.214
  136.9 2.4 scatter_custom_fusion.1
  139.4 2.4 scatter_custom_fusion
  141.9 67.1 %reduce-scatter.4.cloned.1.call-done = bf16[128,2880]{1,0:T(8,128)(2,1)} async-done(((bf16[1024,2880]{1,0:T(8,128)(2,1)}), bf16[128,2880]{1,0:T(8,128)(2,1)}) %reduce-scatter.4.cloned.1.call-update) | async-done | bytes 737296
  209.0 1.5 copy.75
  210.5 0.4 multiply_reduce_fusion.1
  210.9 0.4 copy-done.2
  211.3 0.4 multiply_convert_fusion.1
  211.8 0.3 copy.67
  212.1 1.1 gather_fusion
  213.2 0.1 broadcast_select_fusion
  213.4 0.8 tile.2
  214.2 81.2 %all_to_all.38 = bf16[128,8,2880]{2,1,0:T(8,128)(2,1)S(1)} all-to-all(bf16[128,8,2880]{2,1,0:T(8,128)(2,1)S(1)} %bitcast.86), channel_id=1, replica_groups=mesh['ctx'=8,'exp'=16] {'ctx','exp'}, dimensions={0} | all-to-all | bytes 11796480 | tf_op jit(solution)/shard_map/all_to_all | solution.py:121
  295.3 2.5 fusion.6
  297.8 0.0 copy-start.9
  297.9 2.7 multiply_convert_fusion
  300.6 5.2 %convolution_convert_fusion.1 = bf16[1024,2880]{0,1:T(8,128)(2,1)} fusion(bf16[1024,360]{0,1:T(8,128)(2,1)S(1)} %multiply_convert_fusion, bf16[1,360,2880]{2,1,0:T(8,128)(2,1)S(1)} %copy-done.9), kind=kOutput, calls=%fused_computation.18 | convolution fusion | flops 2126315520 | bytes 8709120 | tf_op jit(solution)/shard_map/dot_general | solution.py:123
  305.8 8.5 %copy.68 = bf16[1024,2880]{1,0:T(8,128)(2,1)} copy(bf16[1024,2880]{0,1:T(8,128)(2,1)} %convolution_convert_fusion.1) | data formatting | bytes 11796480 | tf_op jit(solution)/shard_map/convert_element_type | solution.py:123
  314.3 7.5 %all-to-all-start.2 = ((bf16[128,8,2880]{2,1,0:T(8,128)(2,1)}), bf16[128,8,2880]{2,1,0:T(8,128)(2,1)}, u32[]{:S(2)}, u32[]{:S(2)}) async-start(bf16[128,8,2880]{2,1,0:T(8,128)(2,1)} %bitcast.85), calls=%async_computation.2 | async-start | bytes 12058624 | tf_op jit(solution)/shard_map/all_to_all | solution.py:124
  321.7 0.1 reshape.196
  321.9 77.4 %all-to-all-done.2 = bf16[128,8,2880]{2,1,0:T(8,128)(2,1)} async-done(((bf16[128,8,2880]{2,1,0:T(8,128)(2,1)}), bf16[128,8,2880]{2,1,0:T(8,128)(2,1)}, u32[]{:S(2)}, u32[]{:S(2)}) %all-to-all-start.2) | async-done | bytes 5898272 | tf_op jit(solution)/shard_map/all_to_all | solution.py:124
  399.3 3.5 bitcast_reduce_fusion
  402.8 3.8 gather_fusion.1
  406.6 6.5 %reshape.221 = f32[128,4,2880]{2,1,0:T(4,128)} reshape(bf16[512,2880]{1,0:T(8,128)(2,1)} %gather_fusion.1) | data formatting | bytes 8847360 | tf_op jit(solution)/shard_map/convert_element_type | solution.py:131
  413.1 8.3 %multiply_reduce_fusion = f32[128,2880]{1,0:T(8,128)} fusion(f32[128,4,2880]{2,1,0:T(4,128)} %reshape.221, f32[128,4]{1,0:T(8,128)S(1)} %get-tuple-element.5), kind=kLoop, calls=%fused_computation.16 | loop fusion | flops 2580480 | bytes 7374848 | tf_op jit(solution)/shard_map/reduce_sum | solution.py:133
  421.4 3.0 copy.70
  424.4 2.9 add_convert_fusion
  (34 shorter events, 0.2 us)
Async XLA Ops:
  6.5 113.3 %copy-start = (bf16[512,2880]{0,1:T(8,128)(2,1)S(1)}, bf16[512,2880]{0,1:T(8,128)(2,1)}, u32[]{:S(2)}) copy-start(bf16[512,2880]{0,1:T(8,128)(2,1)} %param.20) | copy-start | bytes 8847364
  6.5 39.5 %all-gather.4.cloned.1.call-start = ((), (), s32[]{:S(2)}) async-start(), calls=%async_computation.4 | async-start | bytes 1179648 | tf_op jit(solution)/shard_map/all_gather | solution.py:45
  7.3 78.4 %all-gather.6.cloned.1.call-start = ((), (), s32[]{:S(2)}) async-start(), calls=%async_computation.5 | async-start | bytes 1179648 | tf_op jit(solution)/shard_map/all_gather | solution.py:46
  8.0 201.0 %reduce-scatter.4.cloned.1.call-start = ((), (), s32[]{:S(2)}) async-start(), calls=%async_computation.6 | async-start | bytes 6782976
  133.4 0.7 copy-start.5
  133.4 0.9 copy-start.6
  133.4 77.1 %copy-start.3 = (bf16[128,2880]{0,1:T(8,128)(2,1)S(1)}, bf16[128,2880]{0,1:T(8,128)(2,1)}, u32[]{:S(2)}) copy-start(bf16[128,2880]{0,1:T(8,128)(2,1)} %param.13) | copy-start | bytes 2211844
  134.1 77.3 %copy-start.4 = (f32[2880]{0:T(1024)S(1)}, f32[2880]{0:T(1024)}, u32[]{:S(2)}) copy-start(f32[2880]{0:T(1024)} %param.19) | copy-start | bytes 34564
  210.5 0.9 copy-start.2
  214.1 81.2 %copy-start.7 = (bf16[1,2880,360]{1,2,0:T(8,128)(2,1)S(1)}, bf16[1,2880,360]{1,2,0:T(8,128)(2,1)}, u32[]{:S(2)}) copy-start(bf16[1,2880,360]{1,2,0:T(8,128)(2,1)} %param.21) | copy-start | bytes 6220804
  295.3 2.5 copy-start.8
  297.8 2.7 copy-start.9
  314.3 85.0 %all-to-all-start.2 = ((bf16[128,8,2880]{2,1,0:T(8,128)(2,1)}), bf16[128,8,2880]{2,1,0:T(8,128)(2,1)}, u32[]{:S(2)}, u32[]{:S(2)}) async-start(bf16[128,8,2880]{2,1,0:T(8,128)(2,1)} %bitcast.85), calls=%async_computation.2 | async-start | bytes 12058624 | tf_op jit(solution)/shard_map/all_to_all | solution.py:124
  413.1 14.2 %copy-start.1 = (bf16[512,2880]{0,1:T(8,128)(2,1)S(1)}, bf16[512,2880]{0,1:T(8,128)(2,1)}, u32[]{:S(2)}) copy-start(bf16[512,2880]{0,1:T(8,128)(2,1)} %param.20) | copy-start | bytes 8847364
Sparse Core Ops, SparseCore 0:
  9.0 37.0 all-gather.3
  47.7 37.9 all-gather.5
  133.5 75.3 reduce-scatter.3
where the time goes:
time: 437 us; the launch traced here: 434 us
  waiting for transfers between devices  172 us (39%)
  blocking collectives  111 us (25%)
  local copies, waits for them, and re-layouts  51.3 us (12%)
  matrix products  45.4 us (10%)
  other arithmetic  33.2 us (8%)
  between operations  13.4 us (3%)
  starting transfers between devices  7.55 us (2%)
    all_to_all x1, blocking collectives, on_device(): lax.all_to_all(copies, ('ctx', 'exp'), split_axis=0, concat_axis=0, tiled...  81.2 us
    all_to_all x1, waiting for transfers between devices, on_device(): lax.all_to_all(partial_value, ('ctx', 'exp'), split_axis=0, concat_axis=0...  77.4 us
    unnamed x4, waiting for transfers between devices  68.5 us
    all_gather x1, waiting for transfers between devices, on_device(): key_section = lax.all_gather(keys, 'ctx', axis=0, tiled=True)  17.7 us
    all_gather x1, blocking collectives, on_device(): doc_piece = lax.all_gather(doc_wire, 'ctx', axis=0, tiled=True)  15.8 us
    dot_general x1, matrix products, on_device(): jnp.einsum('rgjk,kgd->rgjd', prob.astype(jnp.bfloat16), value_section.res...  15.4 us
    dot_general x1, matrix products, on_device(): jnp.einsum('rgjd,kgd->rgjk', query_layout, key_section.reshape(entry_coun...  14.6 us
    reduce_sum x1, other arithmetic, on_device(): softmax_divisor = softmax_divisor * shrink + jnp.sum(prob, axis=-1)  14.3 us
  transfers between devices with their start and end apart: 4, of which 4 were waited for; matrix products, arithmetic and copies ran while one was open for 10% of the time, Pallas kernels for 0%

commit v1 on v0

v1 whole, which is shorter than its diff:
```python
import functools

import jax
import jax.numpy as jnp
from jax import lax
from jax.experimental import pallas as pl
from jax.experimental.pallas import tpu as pltpu
from jax.sharding import PartitionSpec as P

D = 2880
QUERY_HEADS = 64
KEY_VALUE_HEADS = 8
HEAD_SIZE = 64
ALL_EXPERTS = 128
TOPK = 4
CAP = 8
TOK = 128
FFS = 360
NX = 4
QUARTER = ALL_EXPERTS // TOPK
WINDOW = 4
DOC_ROWS = 16
PACK_ROWS = TOK + DOC_ROWS
PACK_COLS = 1280
HALF = D // 2
MIB = 1024 * 1024

VMEM = pltpu.VMEM
ANY = pl.ANY
SMEM = pltpu.SMEM

RIGHT = [(4 * y + x, 4 * y + (x + 1) % 4) for y in range(2) for x in range(4)]
LEFT = [(4 * y + x, 4 * y + (x + 3) % 4) for y in range(2) for x in range(4)]
FLIP = [(c, c ^ 4) for c in range(8)]

NT = (((1,), (1,)), ((), ()))
TN = (((0,), (0,)), ((), ()))


def go_right(v):
    return lax.ppermute(v, "ctx", RIGHT)


def go_left(v):
    return lax.ppermute(v, "ctx", LEFT)


def go_flip(v):
    return lax.ppermute(v, "ctx", FLIP)


def params(mib):
    return pltpu.CompilerParams(vmem_limit_bytes=mib * MIB)


def spec(space):
    return pl.BlockSpec(memory_space=space)


def add(*pieces):
    total = pieces[0].astype(jnp.float32)
    for piece in pieces[1:]:
        total = total + piece.astype(jnp.float32)
    return total.astype(jnp.bfloat16)


def pack_kernel(q_ref, k_ref, v_ref, seg_ref, out_ref):
    lane = lax.broadcasted_iota(jnp.int32, (TOK, 128), 1)
    docs = jnp.broadcast_to(seg_ref[...].astype(jnp.float32), (DOC_ROWS, 128))
    eighth = jnp.asarray(0.125, jnp.bfloat16)
    for x in range(NX):
        out_ref[x, :TOK, 0:512] = q_ref[:, 512 * x : 512 * x + 512] * eighth
        out_ref[x, :TOK, 512:1024] = q_ref[:, 2048 + 512 * x : 2048 + 512 * x + 512] * eighth
        for ref, start in ((k_ref, 1024), (v_ref, 1152)):
            base = 128 * (x // 2)
            low = ref[:, base : base + 128].astype(jnp.float32)
            high = ref[:, 256 + base : 256 + base + 128].astype(jnp.float32)
            if x % 2 == 0:
                high = pltpu.roll(high, 64, 1)
            else:
                low = pltpu.roll(low, 64, 1)
            out_ref[x, :TOK, start : start + 128] = jnp.where(lane < 64, low, high).astype(
                jnp.bfloat16
            )
        out_ref[x, TOK:, 0:1024] = jnp.zeros((DOC_ROWS, 1024), jnp.bfloat16)
        out_ref[x, TOK:, 1024:1152] = docs.astype(jnp.bfloat16)
        out_ref[x, TOK:, 1152:1280] = jnp.zeros((DOC_ROWS, 128), jnp.bfloat16)


def pack(queries, keys, values, segments):
    return pl.pallas_call(
        pack_kernel,
        out_shape=jax.ShapeDtypeStruct((NX, PACK_ROWS, PACK_COLS), jnp.bfloat16),
        in_specs=[spec(VMEM)] * 4,
        out_specs=spec(VMEM),
        compiler_params=params(12),
        cost_estimate=pl.CostEstimate(flops=0, bytes_accessed=5 << 20, transcendentals=0),
    )(queries, keys, values, segments.reshape(1, TOK))


def attend_kernel(steps, sinks, pack_ref, low_ref, out_ref, key_a, key_b, val_a, val_b, doc_row, bias, hold):
    ctx = lax.axis_index("ctx")
    y, x = ctx // NX, lax.rem(ctx, NX)
    lane = lax.broadcasted_iota(jnp.int32, (TOK, 128), 1)

    def place(ref, b, first, slot):
        rows = pl.ds(pl.multiple_of(slot * TOK, TOK), TOK)
        keys = ref[b, 0:TOK, first : first + 128].astype(jnp.float32)
        vals = ref[b, 0:TOK, first + 128 : first + 256].astype(jnp.float32)
        for g in range(2):
            mine = (lane < 64) if g == 0 else (lane >= 64)
            k_here = jnp.where(mine, keys, 0.0)
            v_here = jnp.where(mine, vals, 1.0)
            k_roll = pltpu.roll(k_here, 64, 1)
            v_roll = pltpu.roll(v_here, 64, 1)
            pair_k = (k_here, k_roll) if g == 0 else (k_roll, k_here)
            pair_v = (v_here, v_roll) if g == 0 else (v_roll, v_here)
            key_a[g, rows] = pair_k[0].astype(jnp.bfloat16)
            key_b[g, rows] = pair_k[1].astype(jnp.bfloat16)
            val_a[g, rows] = pair_v[0].astype(jnp.bfloat16)
            val_b[g, rows] = pair_v[1].astype(jnp.bfloat16)
        doc_row[:, rows] = ref[b, TOK : TOK + 8, first : first + 128].astype(jnp.float32)

    for b in range(NX):
        place(pack_ref, b, 1024, 4 * y + b)

    @pl.when(y == 1)
    def _():
        for b in range(NX):
            place(low_ref, b, 0, b)

    two = 2 * TOK
    upper = lax.broadcasted_iota(jnp.int32, (two, 128), 0) < TOK
    first = lax.broadcasted_iota(jnp.int32, (two, 128), 1) < 64

    for index, step in enumerate(steps):
        j = lax.rem(x + step, NX)
        block = 4 * y + j
        own_docs = doc_row[0:1, pl.ds(pl.multiple_of(block * TOK, TOK), TOK)]
        query_docs = jnp.transpose(jnp.broadcast_to(own_docs, (TOK, TOK)))
        query_place = block * TOK + lax.broadcasted_iota(jnp.int32, (TOK, 128), 0)

        def run(chunks, index=index, j=j, query_docs=query_docs, query_place=query_place):
            for t in range(2 * chunks):
                cols = slice(128 * t, 128 * t + 128)
                allowed = (query_docs == doc_row[0:1, cols]) & (128 * t + lane <= query_place)
                bias[:, cols] = jnp.where(allowed, 0.0, -jnp.inf)

            def quad(p, carry):
                g = p // 2
                base = pl.multiple_of(p * 256, 256)
                place_out = pl.multiple_of(512 * lax.rem(g + y, 2) + 256 * lax.rem(p, 2), 256)
                q = jnp.concatenate(
                    [
                        pack_ref[j, 0:TOK, pl.ds(base, 128)],
                        pack_ref[j, 0:TOK, pl.ds(pl.multiple_of(base + 128, 128), 128)],
                    ],
                    axis=0,
                )
                head = 8 * x + 32 * g + 4 * lax.rem(p, 2)
                tops, sink_rows = [], []
                for which, key_ref in enumerate((key_a, key_b)):
                    sink = jnp.where(upper, sinks[head + which], sinks[head + 2 + which])
                    top = sink
                    for c in range(chunks):
                        cols = slice(256 * c, 256 * c + 256)
                        s = lax.dot_general(
                            q, key_ref[g, cols], NT, preferred_element_type=jnp.float32
                        )
                        mask = bias[:, cols]
                        s = s + jnp.concatenate([mask, mask], axis=0)
                        hold[which, :, cols] = s
                        top = jnp.maximum(top, jnp.maximum(s[:, 0:128], s[:, 128:256]))
                    tops.append(jnp.max(top, axis=1, keepdims=True))
                    sink_rows.append(sink)
                outs = []
                for which, val_ref in enumerate((val_a, val_b)):
                    total = jnp.zeros((two, 128), jnp.float32)
                    for c in range(chunks):
                        cols = slice(256 * c, 256 * c + 256)
                        prob = jnp.exp(hold[which, :, cols] - tops[which]).astype(jnp.bfloat16)
                        total = total + jnp.dot(
                            prob, val_ref[g, cols], preferred_element_type=jnp.float32
                        )
                    outs.append(total)
                numer = jnp.where(first, outs[0], outs[1])
                divisor = pltpu.roll(jnp.where(first, outs[1], outs[0]), 64, 1)
                gap = jnp.where(first, sink_rows[0] - tops[0], sink_rows[1] - tops[1])
                result = (numer / (divisor + jnp.exp(gap))).astype(jnp.bfloat16)
                rows = slice(index * TOK, index * TOK + TOK)
                out_ref[rows, pl.ds(place_out, 128)] = result[0:TOK]
                out_ref[rows, pl.ds(pl.multiple_of(place_out + 128, 128), 128)] = result[TOK:]
                return carry

            lax.fori_loop(0, 4, quad, 0)

        for quarter in range(4):

            @pl.when(block // 2 == quarter)
            def _(run=run, quarter=quarter):
                run(quarter + 1)


def attend(steps, sinks, packed, low):
    return pl.pallas_call(
        functools.partial(attend_kernel, steps),
        out_shape=jax.ShapeDtypeStruct((2 * TOK, 1024), jnp.bfloat16),
        in_specs=[spec(SMEM), spec(VMEM), spec(VMEM)],
        out_specs=spec(VMEM),
        scratch_shapes=[
            pltpu.VMEM((2, 1024, 128), jnp.bfloat16),
            pltpu.VMEM((2, 1024, 128), jnp.bfloat16),
            pltpu.VMEM((2, 1024, 128), jnp.bfloat16),
            pltpu.VMEM((2, 1024, 128), jnp.bfloat16),
            pltpu.VMEM((8, 1024), jnp.float32),
            pltpu.VMEM((TOK, 1024), jnp.float32),
            pltpu.VMEM((2, 2 * TOK, 1024), jnp.float32),
        ],
        compiler_params=params(20),
        cost_estimate=pl.CostEstimate(
            flops=2 << 30, bytes_accessed=4 << 20, transcendentals=0
        ),
    )(sinks, packed, low)


def project_kernel(finish, attn, w_own, w_first, w_second, *refs):
    core = lax.rem(lax.axis_index("exp"), 2)
    if finish:
        plus_a, ra, lb = refs[:3]
        to_right, left_a, left_b, right_a, right_b = refs[3:]
        to_right[...] = add(plus_a[...], ra[...])
    else:
        left_a, left_b, right_a, right_b = refs
    for w_near, base, left_out, right_out in (
        (w_first, core * HALF, left_a, right_a),
        (w_second, (1 - core) * HALF, left_b, right_b),
    ):
        for start in range(0, HALF, 288):
            near = slice(start, start + 288)
            rows = pl.ds(pl.multiple_of(base + start, 16), 288)
            total = lax.dot_general(
                w_own[rows], attn[:, 0:512], NT, preferred_element_type=jnp.float32
            ) + lax.dot_general(
                w_near[near], attn[:, 512:1024], NT, preferred_element_type=jnp.float32
            )
            left = total[:, 0:128]
            if finish and left_out is left_b:
                left = left + lb[near].astype(jnp.float32)
            left_out[near] = left.astype(jnp.bfloat16)
            right_out[near] = total[:, 128:256].astype(jnp.bfloat16)


def project(attn, w_own, w_first, w_second, *extra):
    finish = len(extra) > 0
    count = 5 if finish else 4
    return pl.pallas_call(
        functools.partial(project_kernel, finish),
        out_shape=(jax.ShapeDtypeStruct((HALF, TOK), jnp.bfloat16),) * count,
        in_specs=[spec(VMEM)] * (4 + len(extra)),
        out_specs=(spec(VMEM),) * count,
        compiler_params=params(20),
        cost_estimate=pl.CostEstimate(flops=3 << 29, bytes_accessed=4 << 20, transcendentals=0),
    )(attn, w_own, w_first, w_second, *extra)


def slot_table(ids):
    local = ids % QUARTER
    chosen = jnp.where(local < WINDOW, ids // QUARTER * WINDOW + local, -1)
    slot = lax.broadcasted_iota(jnp.int32, (TOK, TOK), 0)
    expert = slot // CAP
    hits = [chosen[k : k + 1] == expert for k in range(TOPK)]
    named = functools.reduce(jnp.logical_or, hits)
    before = lax.broadcasted_iota(jnp.int32, (TOK, TOK), 0) < lax.broadcasted_iota(
        jnp.int32, (TOK, TOK), 1
    )
    rank = jnp.dot(
        jnp.where(named, 1.0, 0.0).astype(jnp.bfloat16),
        jnp.where(before, 1.0, 0.0).astype(jnp.bfloat16),
        preferred_element_type=jnp.float32,
    )
    table = named & (rank == (slot % CAP).astype(jnp.float32))
    return table, hits


def norm_kernel(
    resid, own_a, own_b, left_a, left_b, right_a, right_b, gain, ids, hidden_ref, send_ref, gain_row
):
    core = lax.rem(lax.axis_index("exp"), 2)
    gain_row[...] = jnp.ones_like(gain_row)
    gain_row[:, 0:D] = gain[...]
    square = jnp.zeros((8, TOK), jnp.float32)
    for base, own, left, right in (
        (core * HALF, own_a, left_a, right_a),
        ((1 - core) * HALF, own_b, left_b, right_b),
    ):
        for start in range(0, HALF, 160):
            near = slice(start, start + 160)
            rows = pl.ds(pl.multiple_of(base + start, 16), 160)
            total = own[near].astype(jnp.float32)
            total = total + left[near].astype(jnp.float32) + right[near].astype(jnp.float32)
            hidden = resid[rows].astype(jnp.float32) + total
            hidden_ref[rows] = hidden
            square = square + jnp.sum((hidden * hidden).reshape(20, 8, TOK), axis=0)
    mean = jnp.sum(square, axis=0, keepdims=True) * (1.0 / D)
    scale = lax.rsqrt(mean + 1e-05)
    table, _ = slot_table(ids[...])
    table = jnp.where(table, 1.0, 0.0).astype(jnp.bfloat16)
    for start in range(0, D, 128):
        size = min(128, D - start)
        rows = slice(start, start + size)
        gains = jnp.transpose(jnp.broadcast_to(gain_row[:, start : start + 128], (128, 128)))
        normed = (hidden_ref[rows] * scale * gains[0:size]).astype(jnp.bfloat16)
        send_ref[:, rows] = lax.dot_general(
            table, normed, NT, preferred_element_type=jnp.float32
        ).astype(jnp.bfloat16)


def norm(resid, own_a, own_b, left_a, left_b, right_a, right_b, gain, ids):
    return pl.pallas_call(
        norm_kernel,
        out_shape=(
            jax.ShapeDtypeStruct((D, TOK), jnp.float32),
            jax.ShapeDtypeStruct((TOK, D), jnp.bfloat16),
        ),
        in_specs=[spec(VMEM)] * 9,
        out_specs=(spec(VMEM), spec(VMEM)),
        scratch_shapes=[pltpu.VMEM((1, D + 64), jnp.float32)],
        compiler_params=params(16),
        cost_estimate=pl.CostEstimate(flops=1 << 27, bytes_accessed=6 << 20, transcendentals=0),
    )(resid, own_a, own_b, left_a, left_b, right_a, right_b, gain, ids)


def combine_kernel(hidden, back, ids, weights, out_ref):
    table, hits = slot_table(ids[...])
    chosen_weight = jnp.zeros((TOK, TOK), jnp.float32)
    for k in range(TOPK):
        chosen_weight = chosen_weight + jnp.where(hits[k], weights[k : k + 1], 0.0)
    share = jnp.where(table, chosen_weight, 0.0)
    high = share.astype(jnp.bfloat16)
    low = (share - high.astype(jnp.float32)).astype(jnp.bfloat16)
    for start in range(0, D, 128):
        cols = slice(start, min(start + 128, D))
        rows = back[:, cols]
        moe = lax.dot_general(rows, high, TN, preferred_element_type=jnp.float32)
        moe = moe + lax.dot_general(rows, low, TN, preferred_element_type=jnp.float32)
        out_ref[cols] = (hidden[cols] + moe).astype(jnp.bfloat16)


def combine(hidden, back, ids, weights):
    return pl.pallas_call(
        combine_kernel,
        out_shape=jax.ShapeDtypeStruct((D, TOK), jnp.bfloat16),
        in_specs=[spec(VMEM)] * 4,
        out_specs=spec(VMEM),
        compiler_params=params(16),
        cost_estimate=pl.CostEstimate(flops=1 << 28, bytes_accessed=3 << 20, transcendentals=0),
    )(hidden, back, ids, weights)


LOADS = ((2, 3), (4, 5), (7, 8))


def expert_kernel(sizes, *refs):
    count = len(sizes)
    pieces, weights, outs = refs[:count], refs[count : count + 9], refs[count + 9 : 2 * count + 9]
    rows_x, held, sem = refs[2 * count + 9], refs[2 * count + 10 : 2 * count + 13], refs[-1]
    core = lax.rem(lax.axis_index("exp"), 2)
    copies = []
    start = 0
    for index, (piece, size) in enumerate(zip(pieces, sizes)):
        copies.append(
            pltpu.make_async_copy(piece, rows_x.at[pl.ds(start, size)], sem.at[index])
        )
        start += size
    loads = []
    for index, (group, dst) in enumerate(zip(LOADS, held)):
        loads.append(
            [pltpu.make_async_copy(weights[w], dst, sem.at[count + index]) for w in group]
        )

    def each(load, act):
        for which, copy in enumerate(load):

            @pl.when(core == which)
            def _(copy=copy):
                act(copy)

    def start_load(load):
        each(load, lambda copy: copy.start())

    def wait_load(load):
        each(load, lambda copy: copy.wait())

    for copy in copies:
        copy.start()
    for load in loads:
        start_load(load)
    for copy in copies:
        copy.wait()
    x = rows_x[...]
    gate_own, up_own, down_own = weights[0], weights[1], weights[6]
    gate_near, up_near, down_near = held

    def hidden_units(gate, up, ready):
        g = lax.dot_general(x, gate[...], NT, preferred_element_type=jnp.float32)
        ready()
        v = lax.dot_general(x, up[...], NT, preferred_element_type=jnp.float32)
        return ((v + 1.0) * g * jax.nn.sigmoid(1.702 * g)).astype(jnp.bfloat16)

    act_own = hidden_units(gate_own, up_own, lambda: None)
    wait_load(loads[0])
    act_near = hidden_units(gate_near, up_near, lambda: wait_load(loads[1]))
    wait_load(loads[2])
    for first in range(0, D, 512):
        cols = slice(first, min(first + 512, D))
        part = jnp.dot(act_own, down_own[:, cols], preferred_element_type=jnp.float32)
        part = part + jnp.dot(act_near, down_near[:, cols], preferred_element_type=jnp.float32)
        part = part.astype(jnp.bfloat16)
        start = 0
        for out, size in zip(outs, sizes):
            out[:, cols] = part[start : start + size]
            start += size


def experts(pieces, weights):
    sizes = tuple(piece.shape[0] for piece in pieces)
    total = sum(sizes)
    return pl.pallas_call(
        functools.partial(expert_kernel, sizes),
        out_shape=tuple(jax.ShapeDtypeStruct((size, D), jnp.bfloat16) for size in sizes),
        in_specs=[spec(ANY)] * len(sizes)
        + [spec(VMEM)] * 2
        + [spec(ANY)] * 4
        + [spec(VMEM)]
        + [spec(ANY)] * 2,
        out_specs=tuple(spec(VMEM) for _ in sizes),
        scratch_shapes=[pltpu.VMEM((total, D), jnp.bfloat16)]
        + [pltpu.VMEM((FFS, D), jnp.bfloat16)] * 3
        + [pltpu.SemaphoreType.DMA((len(sizes) + 3,))],
        compiler_params=params(32),
        cost_estimate=pl.CostEstimate(
            flops=12 * total * D * FFS, bytes_accessed=14 << 20, transcendentals=2 * total * FFS
        ),
    )(*pieces, *weights)


def over_all(move):
    pairs = []
    for c in range(8):
        for e in range(16):
            y, x, z, hi, core = move(c // 4, c % 4, e // 4, e // 2 % 2, e % 2)
            pairs.append((c * 16 + e, (y * 4 + x) * 16 + z * 4 + hi * 2 + core))
    return pairs


def partner(y, x, z, hi, core):
    return (1 - y, x, z, hi, core) if core == 0 else (y, x ^ 1, z, hi, core)


def onward(y, x, z, hi, core):
    if core == 0:
        return y, (x + 1) % 4, z, hi, core
    across = x < 2 if y == 0 else x >= 2
    return (y, 3 - x, z, hi, core) if across else (1 - y, x, z, hi, core)


def across_y(y, x, z, hi, core):
    place = (2 * hi + y + (1 if y == 1 else 3)) % 4
    return place % 2, x, z, place // 2, core


def permute(v, pairs):
    return lax.ppermute(v, ("ctx", "exp"), pairs)


NEXT = over_all(onward)
BACK = [(b, a) for a, b in NEXT]
PARTNER = [[(a, b) for a, b in over_all(partner) if a % 2 == core] for core in range(2)]
ACROSS = over_all(across_y)
SWAP = over_all(lambda y, x, z, hi, core: (y, x, z, hi, 1 - core))


def exchange_experts(arrived, weights):
    half = TOK // 2
    own_a, own_b = arrived[:half], arrived[half:]
    prev_a, next_b = permute(own_a, NEXT), permute(own_b, BACK)
    prev_b, next_a = permute(own_b, NEXT), permute(own_a, BACK)
    opp_a, opp_b = permute(prev_a, NEXT), permute(next_b, BACK)
    oo_a, oo_b, op_a, op_b, on_a, on_b = experts(
        (own_a, own_b, prev_a, prev_b, next_a, next_b), weights
    )
    opp_a, opp_b, oo_a, oo_b, op_a, op_b, on_a, on_b = lax.optimization_barrier(
        (opp_a, opp_b, oo_a, oo_b, op_a, op_b, on_a, on_b)
    )
    far_a, far_b = experts((opp_a, opp_b), weights)
    on_at_next, op_at_prev = permute(far_a, NEXT), permute(far_b, BACK)
    got_b, got_a = permute(on_b, NEXT), permute(op_a, BACK)
    more_a = permute(add(on_a, on_at_next), NEXT)
    more_b = permute(add(op_b, op_at_prev), BACK)
    return jnp.concatenate([add(oo_a, got_a, more_a), add(oo_b, got_b, more_b)], axis=0)


def on_device(
    resid_in,
    queries,
    keys,
    values,
    sinks,
    segments,
    norm_gain,
    out_weight,
    gate_weight,
    up_weight,
    down_weight,
    expert_ids,
    route_weights,
):
    core = lax.axis_index("exp") % 2
    gate, up, down = gate_weight[0].T, up_weight[0].T, down_weight[0]
    w_own = out_weight.T

    mine = lax.dynamic_slice_in_dim(w_own, core * (D // 2), D // 2, 0)
    w_first = permute(mine, ACROSS)
    gate_0 = permute(gate, PARTNER[0])

    packed = pack(queries, keys, values, segments)
    packed = lax.all_to_all(
        packed,
        "ctx",
        split_axis=0,
        concat_axis=0,
        tiled=True,
        axis_index_groups=[[0, 1, 2, 3], [4, 5, 6, 7]],
    )
    packed, gate_0, gate_out = lax.optimization_barrier((packed, gate_0, gate))
    low = lax.ppermute(packed[:, :, 1024:], "ctx", [(x, x + 4) for x in range(4)])
    gate_1 = permute(gate_out, PARTNER[1])
    low, w_first, up_out, down_out = lax.optimization_barrier((low, w_first, up, down))
    w_second = permute(w_first, SWAP)
    up_0, down_0 = permute(up_out, PARTNER[0]), permute(down_out, PARTNER[0])

    attn = attend((2, 1), sinks, packed, low)
    opp_a, opp_b, plus_a, plus_b = project(attn, w_own, w_first, w_second)
    ra, lb, right_b = go_right(opp_a), go_left(opp_b), go_right(plus_b)
    attn = attend((3, 0), sinks, packed, low)
    attn, gate_1, up_0 = lax.optimization_barrier((attn, gate_1, up_0))
    to_right, to_left_a, to_left_b, own_a, own_b = project(
        attn, w_own, w_first, w_second, plus_a, ra, lb
    )
    right_a, left_a, left_b = go_right(to_right), go_left(to_left_a), go_left(to_left_b)

    right_a, right_b, left_a, left_b, up_out, down_out = lax.optimization_barrier(
        (right_a, right_b, left_a, left_b, up, down)
    )
    up_1, down_1 = permute(up_out, PARTNER[1]), permute(down_out, PARTNER[1])

    ids = expert_ids.T
    hidden, send = norm(
        resid_in.T, own_a, own_b, right_a, right_b, left_a, left_b, norm_gain.reshape(1, D), ids
    )
    send, down_0 = lax.optimization_barrier((send, down_0))
    arrived = lax.all_to_all(send, "exp", split_axis=0, concat_axis=0, tiled=True)
    arrived, up_1 = lax.optimization_barrier((arrived, up_1))
    summed = exchange_experts(
        arrived, (gate, up, gate_0, gate_1, up_0, up_1, down, down_0, down_1)
    )
    back = lax.all_to_all(summed, "exp", split_axis=0, concat_axis=0, tiled=True)
    return combine(hidden, back, ids, route_weights.T).T


def solution(mesh):
    placed = (
        P(("exp", "ctx"), None),
        P(("exp", "ctx"), None),
        P(("exp", "ctx"), None),
        P(("exp", "ctx"), None),
        P(),
        P(("exp", "ctx")),
        P(),
        P("ctx", None),
        P("exp", None, "ctx"),
        P("exp", None, "ctx"),
        P("exp", "ctx", None),
        P(("exp", "ctx"), None),
        P(("exp", "ctx"), None),
    )
    return jax.shard_map(
        on_device, mesh=mesh, in_specs=placed, out_specs=P(("exp", "ctx"), None), check_vma=False
    )
```

time: 437 us -> 208 us (0.48)
  waiting for transfers between devices: 172 us -> 49.5 us
  local copies, waits for them, and re-layouts: 51.3 us -> 4.54 us
  matrix products: 45.4 us -> 0 us
  blocking collectives: 111 us -> 66.4 us
  starting transfers between devices: 7.55 us -> 51.5 us
  Pallas kernels: 0 us -> 33.4 us
  other arithmetic: 33.2 us -> 0.52 us
  between operations: 13.4 us -> 0.35 us
    all_to_all x1 -> x0, waiting for transfers between devices: 77.4 us -> none  [on_device(): lax.all_to_all(partial_value, ('ctx', 'exp'), split_axis=0, concat_axis=0...]
    unnamed x4 -> x0, waiting for transfers between devices: 68.5 us -> none
    ppermute x0 -> x27, starting transfers between devices: none -> 51.5 us  [the longest x20 42.6 us: permute(): return lax.ppermute(v, ('ctx', 'exp'), pairs)]
    ppermute x0 -> x27, waiting for transfers between devices: none -> 49.5 us  [the longest x20 37.2 us: permute(): return lax.ppermute(v, ('ctx', 'exp'), pairs)]
    dot_general x6 -> x0, matrix products: 45.4 us -> none  [the longest x1 15.4 us: on_device(): jnp.einsum('rgjk,kgd->rgjd', prob.astype(jnp.bfloat16), value_section.res...]
    pallas_call x0 -> x9, Pallas kernels: none -> 33.4 us  [the longest x2 15 us: experts(): pl.pallas_call(functools.partial(expert_kernel, sizes), out_shape=tuple((...]
    all_to_all x2 -> x3, blocking collectives: 95.3 us -> 66.4 us  [the longest x1 27.1 us: on_device(): lax.all_to_all(send, 'exp', split_axis=0, concat_axis=0, tiled=True)]
    reduce_sum x5 -> x0, other arithmetic: 26.7 us -> none  [the longest x1 14.3 us: on_device(): softmax_divisor = softmax_divisor * shrink + jnp.sum(prob, axis=-1)]
  transfers between devices with their start and end apart: 4 -> 27, of which waited for: 4 -> 12; matrix products, arithmetic and copies ran while one was open for 10% -> 1% of each run, Pallas kernels for 0% -> 13%
where the time goes in v1:
time: 208 us; the launch traced here: 206 us
  blocking collectives  66.4 us (32%)
  starting transfers between devices  51.5 us (25%)
  waiting for transfers between devices  49.5 us (24%)
  Pallas kernels  33.4 us (16%)
  local copies, waits for them, and re-layouts  4.54 us (2%)
    ppermute x20, starting transfers between devices, permute(): return lax.ppermute(v, ('ctx', 'exp'), pairs)  42.6 us
    ppermute x20, waiting for transfers between devices, permute(): return lax.ppermute(v, ('ctx', 'exp'), pairs)  37.2 us
    all_to_all x1, blocking collectives, on_device(): lax.all_to_all(send, 'exp', split_axis=0, concat_axis=0, tiled=True)  27.1 us
    all_to_all x1, blocking collectives, on_device(): lax.all_to_all(packed, 'ctx', split_axis=0, concat_axis=0, tiled=True, ax...  20.5 us
    all_to_all x1, blocking collectives, on_device(): lax.all_to_all(summed, 'exp', split_axis=0, concat_axis=0, tiled=True)  18.8 us
    pallas_call x2, Pallas kernels, experts(): pl.pallas_call(functools.partial(expert_kernel, sizes), out_shape=tuple((...  15 us
    pallas_call x2, Pallas kernels, attend(): pl.pallas_call(functools.partial(attend_kernel, steps), out_shape=jax.Sha...  11.7 us
    ppermute x3, waiting for transfers between devices, go_left(): return lax.ppermute(v, 'ctx', LEFT)  10.5 us
  transfers between devices with their start and end apart: 27, of which 12 were waited for; matrix products, arithmetic and copies ran while one was open for 1% of the time, Pallas kernels for 13%

profile of v1, /device:TPU:1, one launch (start us, length us, event | category | flops | bytes accessed | tf_op | source)
XLA Modules:
  0.0 206.2 jit_solution(4680966136429216665)
XLA Ops:
  0.0 0.9 collective-permute-start
  1.0 1.5 dynamic-slice_bitcast_fusion
  2.4 3.6 %collective-permute-start.2 = (bf16[1440,512]{1,0:T(8,128)(2,1)S(1)}, bf16[1440,512]{1,0:T(8,128)(2,1)S(1)}, u32[]{:S(2)}, u32[]{:S(2)}) collective-permute-start(bf16[1440,512]{1,0:T(8,128)(2,1)S(1)} %dynamic-slice_bitcast_fusion), channel_id=1, source_target_pairs={{0,66},{1,67},{2,64},{3,65},{4,70},{5,71},{6,68},{7,69},{8,74},{9,... | collective-permute-start | bytes 4423688 | tf_op jit(solution)/shard_map/ppermute | solution.py:473
  6.1 0.0 copy-start.2
  6.1 0.2 shard_map.127
  6.3 0.0 copy-start.1
  6.4 0.0 copy-start.13
  6.4 20.5 %all_to_all.28.pack_ref = bf16[4,144,1280]{2,1,0:T(8,128)(2,1)S(1)} all-to-all(bf16[4,144,1280]{2,1,0:T(8,128)(2,1)S(1)} %shard_map.127), channel_id=1, replica_groups={{0,16,32,48},{64,80,96,112},{1,17,33,49},{65,81,97,113},{2,18,34,50},{6..., dimensions={0} | all-to-all | bytes 2949120 | tf_op jit(solution)/shard_map/all_to_all | solution.py:527
  26.9 0.0 collective-permute-done.refs_8_.refs_4_
  26.9 1.3 collective-permute-start.1
  28.3 2.3 %collective-permute-start.3 = (bf16[360,2880]{1,0:T(8,128)(2,1)S(1)}, bf16[360,2880]{1,0:T(8,128)(2,1)S(1)}, u32[]{:S(2)}, u32[]{:S(2)}) collective-permute-start(bf16[360,2880]{1,0:T(8,128)(2,1)S(1)} %bitcast.23), channel_id=1, source_target_pairs={{1,17},{3,19},{5,21},{7,23},{9,25},{11,27},{13,29},{15,31},{17,1},... | collective-permute-start | bytes 6220808 | tf_op jit(solution)/shard_map/ppermute | solution.py:473
  30.6 4.5 %collective-permute-done.2.w_first = bf16[1440,512]{1,0:T(8,128)(2,1)S(1)} collective-permute-done((bf16[1440,512]{1,0:T(8,128)(2,1)S(1)}, bf16[1440,512]{1,0:T(8,128)(2,1)S(1)}, u32[]{:S(2)}, u32[]{:S(2)}) %collective-permute-start.2) | collective-permute-done | bytes 1474592 | tf_op jit(solution)/shard_map/ppermute | solution.py:473
  35.1 0.0 collective-permute-done.1.low_ref
  35.1 0.9 collective-permute-start.4
  36.1 6.4 %collective-permute-start.5 = (bf16[1440,512]{1,0:T(8,128)(2,1)S(1)}, bf16[1440,512]{1,0:T(8,128)(2,1)S(1)}, u32[]{:S(2)}, u32[]{:S(2)}) collective-permute-start(bf16[1440,512]{1,0:T(8,128)(2,1)S(1)} %collective-permute-done.2.w_first), channel_id=1, source_target_pairs={{0,1},{1,0},{2,3},{3,2},{4,5},{5,4},{6,7},{7,6},{8,9},{9,8},{10,11... | collective-permute-start | bytes 4423688 | tf_op jit(solution)/shard_map/ppermute | solution.py:473
  42.5 5.8 %shard_map.129.attn = bf16[256,1024]{1,0:T(8,128)(2,1)S(1)} custom-call(f32[64]{0:T(128)S(1)} %copy-done.13, bf16[4,144,1280]{2,1,0:T(8,128)(2,1)S(1)} %all_to_all.28.pack_ref, bf16[4,144,256]{2,1,0:T(8,128)(2,1)S(1)} %collective-permute-done.1.low_ref), custom_call_target="tpu_custom_call" | custom-call | flops 2147483648 | bytes 4194304 | tf_op jit(solution)/shard_map/pallas_call | solution.py:205
  48.3 0.0 copy-start.3
  48.3 1.8 shard_map.130
  50.1 2.5 %collective-permute-start.6 = (bf16[1440,128]{1,0:T(8,128)(2,1)S(1)}, bf16[1440,128]{1,0:T(8,128)(2,1)S(1)}, u32[]{:S(2)}, u32[]{:S(2)}) collective-permute-start(bf16[1440,128]{1,0:T(8,128)(2,1)S(1)} %get-tuple-element.59), channel_id=1, source_target_pairs={{0,16},{16,32},{32,48},{48,0},{64,80},{80,96},{96,112},{112,64},{1... | collective-permute-start | bytes 1105928 | tf_op jit(solution)/shard_map/ppermute | solution.py:41
  52.6 1.2 collective-permute-start.7
  53.8 0.8 collective-permute-start.12
  54.6 6.0 %shard_map.128.attn = bf16[256,1024]{1,0:T(8,128)(2,1)S(1)} custom-call(f32[64]{0:T(128)S(1)} %copy-done.13, bf16[4,144,1280]{2,1,0:T(8,128)(2,1)S(1)} %all_to_all.28.pack_ref, bf16[4,144,256]{2,1,0:T(8,128)(2,1)S(1)} %collective-permute-done.1.low_ref), custom_call_target="tpu_custom_call" | custom-call | flops 2147483648 | bytes 4194304 | tf_op jit(solution)/shard_map/pallas_call | solution.py:205
  60.6 0.3 collective-permute-start.9
  60.9 1.8 collective-permute-done.6.refs_1_
  62.7 0.5 collective-permute-done.7.refs_2_
  63.2 1.9 shard_map.131
  65.2 2.1 %collective-permute-start.10 = (bf16[1440,128]{1,0:T(8,128)(2,1)S(1)}, bf16[1440,128]{1,0:T(8,128)(2,1)S(1)}, u32[]{:S(2)}, u32[]{:S(2)}) collective-permute-start(bf16[1440,128]{1,0:T(8,128)(2,1)S(1)} %get-tuple-element.65), channel_id=1, source_target_pairs={{0,48},{16,0},{32,16},{48,32},{64,112},{80,64},{96,80},{112,96},{1... | collective-permute-start | bytes 1105928 | tf_op jit(solution)/shard_map/ppermute | solution.py:45
  67.2 0.1 collective-permute-start.11
  67.3 1.4 collective-permute-start.8
  68.7 3.2 %collective-permute-done.10.right_a = bf16[1440,128]{1,0:T(8,128)(2,1)S(1)} collective-permute-done((bf16[1440,128]{1,0:T(8,128)(2,1)S(1)}, bf16[1440,128]{1,0:T(8,128)(2,1)S(1)}, u32[]{:S(2)}, u32[]{:S(2)}) %collective-permute-start.10) | collective-permute-done | bytes 368672 | tf_op jit(solution)/shard_map/ppermute | solution.py:45
  71.9 6.7 %collective-permute-done.11.right_b = bf16[1440,128]{1,0:T(8,128)(2,1)S(1)} collective-permute-done((bf16[1440,128]{1,0:T(8,128)(2,1)S(1)}, bf16[1440,128]{1,0:T(8,128)(2,1)S(1)}, u32[]{:S(2)}, u32[]{:S(2)}) %collective-permute-start.11) | collective-permute-done | bytes 368672 | tf_op jit(solution)/shard_map/ppermute | solution.py:45
  78.6 2.8 %collective-permute-start.13 = (bf16[360,2880]{1,0:T(8,128)(2,1)S(1)}, bf16[360,2880]{1,0:T(8,128)(2,1)S(1)}, u32[]{:S(2)}, u32[]{:S(2)}) collective-permute-start(bf16[360,2880]{1,0:T(8,128)(2,1)S(1)} %bitcast.27), channel_id=1, source_target_pairs={{1,17},{3,19},{5,21},{7,23},{9,25},{11,27},{13,29},{15,31},{17,1},... | collective-permute-start | bytes 6220808 | tf_op jit(solution)/shard_map/ppermute | solution.py:473
  81.4 2.5 %collective-permute-start.20 = (bf16[360,2880]{1,0:T(8,128)(2,1)S(1)}, bf16[360,2880]{1,0:T(8,128)(2,1)S(1)}, u32[]{:S(2)}, u32[]{:S(2)}) collective-permute-start(bf16[360,2880]{1,0:T(8,128)(2,1)S(1)} %bitcast.31), channel_id=1, source_target_pairs={{1,17},{3,19},{5,21},{7,23},{9,25},{11,27},{13,29},{15,31},{17,1},... | collective-permute-start | bytes 6220808 | tf_op jit(solution)/shard_map/ppermute | solution.py:473
  84.0 1.2 shard_map.132
  85.2 27.1 %all_to_all.29 = bf16[16,8,2880]{2,1,0:T(8,128)(2,1)S(1)} all-to-all(bf16[16,8,2880]{2,1,0:T(8,128)(2,1)S(1)} %bitcast.35), channel_id=1, replica_groups=mesh['ctx'=8,'exp'=16] {'exp'}, dimensions={0} | all-to-all | bytes 1474560 | tf_op jit(solution)/shard_map/all_to_all | solution.py:562
  112.3 0.1 fusion
  112.3 4.1 %collective-permute-start.14 = (bf16[64,2880]{1,0:T(8,128)(2,1)S(1)}, bf16[64,2880]{1,0:T(8,128)(2,1)S(1)}, u32[]{:S(2)}, u32[]{:S(2)}) collective-permute-start(bf16[64,2880]{1,0:T(8,128)(2,1)S(1)} %get-tuple-element.100.refs_0_), channel_id=1, source_target_pairs={{0,16},{1,49},{2,18},{3,51},{4,20},{5,53},{6,22},{7,55},{8,24},{9,... | collective-permute-start | bytes 1105928 | tf_op jit(solution)/shard_map/ppermute | solution.py:473
  116.5 2.7 %collective-permute-start.18 = (bf16[64,2880]{1,0:T(8,128)(2,1)S(1)}, bf16[64,2880]{1,0:T(8,128)(2,1)S(1)}, u32[]{:S(2)}, u32[]{:S(2)}) collective-permute-start(bf16[64,2880]{1,0:T(8,128)(2,1)S(1)} %get-tuple-element.99.refs_1_), channel_id=1, source_target_pairs={{0,16},{1,49},{2,18},{3,51},{4,20},{5,53},{6,22},{7,55},{8,24},{9,... | collective-permute-start | bytes 1105928 | tf_op jit(solution)/shard_map/ppermute | solution.py:473
  119.2 4.4 %collective-permute-done.14.refs_2_ = bf16[64,2880]{1,0:T(8,128)(2,1)S(1)} collective-permute-done((bf16[64,2880]{1,0:T(8,128)(2,1)S(1)}, bf16[64,2880]{1,0:T(8,128)(2,1)S(1)}, u32[]{:S(2)}, u32[]{:S(2)}) %collective-permute-start.14) | collective-permute-done | bytes 368672 | tf_op jit(solution)/shard_map/ppermute | solution.py:473
  123.6 3.4 %collective-permute-start.15 = (bf16[64,2880]{1,0:T(8,128)(2,1)S(1)}, bf16[64,2880]{1,0:T(8,128)(2,1)S(1)}, u32[]{:S(2)}, u32[]{:S(2)}) collective-permute-start(bf16[64,2880]{1,0:T(8,128)(2,1)S(1)} %collective-permute-done.14.refs_2_), channel_id=1, source_target_pairs={{0,16},{1,49},{2,18},{3,51},{4,20},{5,53},{6,22},{7,55},{8,24},{9,... | collective-permute-start | bytes 1105928 | tf_op jit(solution)/shard_map/ppermute | solution.py:473
  127.0 1.5 collective-permute-done.16.refs_5_
  128.5 10.6 %collective-permute-done.20.refs_14_.refs_10_ = bf16[360,2880]{1,0:T(8,128)(2,1)S(1)} collective-permute-done((bf16[360,2880]{1,0:T(8,128)(2,1)S(1)}, bf16[360,2880]{1,0:T(8,128)(2,1)S(1)}, u32[]{:S(2)}, u32[]{:S(2)}) %collective-permute-start.20) | collective-permute-done | bytes 2073632 | tf_op jit(solution)/shard_map/ppermute | solution.py:473
  139.1 1.3 copy-done.4
  140.4 9.8 %shard_map.133 = (bf16[64,2880]{1,0:T(8,128)(2,1)S(1)}, bf16[64,2880]{1,0:T(8,128)(2,1)S(1)}, bf16[64,2880]{1,0:T(8,128)(2,1)S(1)}, bf16[64,2880]{1,0:T(8,128)(2...) custom-call(bf16[64,2880]{1,0:T(8,128)(2,1)S(1)} %get-tuple-element.100.refs_0_, ...), custom_call_target="tpu_custom_call" | custom-call | flops 4777574400 | bytes 14680064 | tf_op jit(solution)/shard_map/pallas_call | solution.py:428
  150.3 1.6 copy-done.5
  151.9 5.2 %shard_map.134 = (bf16[64,2880]{1,0:T(8,128)(2,1)S(1)}, bf16[64,2880]{1,0:T(8,128)(2,1)S(1)}) custom-call(bf16[64,2880]{1,0:T(8,128)(2,1)S(1)} %collective-permute-done.15.refs_0_, bf16[64,2880]{1,0:T(8,128)(2,1)S(1)} %collective-permute-done.17.refs_1_, bf16[360,2880]{1,0:T(8,128)(2,1)S(1)} %bitcast.25, bf16[360,2880]{1,0:T(8,128)(2,1)S(1)} %bitcast.29, ...), custom_call_target="tpu_custom_call" | custom-call | flops 1592524800 | bytes 14680064 | tf_op jit(solution)/shard_map/pallas_call | solution.py:428
  157.1 2.3 %collective-permute-start.22 = (bf16[64,2880]{1,0:T(8,128)(2,1)S(1)}, bf16[64,2880]{1,0:T(8,128)(2,1)S(1)}, u32[]{:S(2)}, u32[]{:S(2)}) collective-permute-start(bf16[64,2880]{1,0:T(8,128)(2,1)S(1)} %get-tuple-element.94), channel_id=1, source_target_pairs={{0,16},{1,49},{2,18},{3,51},{4,20},{5,53},{6,22},{7,55},{8,24},{9,... | collective-permute-start | bytes 1105928 | tf_op jit(solution)/shard_map/ppermute | solution.py:473
  159.4 3.8 %collective-permute-start.21 = (bf16[64,2880]{1,0:T(8,128)(2,1)S(1)}, bf16[64,2880]{1,0:T(8,128)(2,1)S(1)}, u32[]{:S(2)}, u32[]{:S(2)}) collective-permute-start(bf16[64,2880]{1,0:T(8,128)(2,1)S(1)} %get-tuple-element.90), channel_id=1, source_target_pairs={{16,0},{49,1},{18,2},{51,3},{20,4},{53,5},{22,6},{55,7},{24,8},{57... | collective-permute-start | bytes 1105928 | tf_op jit(solution)/shard_map/ppermute | solution.py:473
  163.2 2.6 %collective-permute-start.25 = (bf16[64,2880]{1,0:T(8,128)(2,1)S(1)}, bf16[64,2880]{1,0:T(8,128)(2,1)S(1)}, u32[]{:S(2)}, u32[]{:S(2)}) collective-permute-start(bf16[64,2880]{1,0:T(8,128)(2,1)S(1)} %get-tuple-element.98), channel_id=1, source_target_pairs={{16,0},{49,1},{18,2},{51,3},{20,4},{53,5},{22,6},{55,7},{24,8},{57... | collective-permute-start | bytes 1105928 | tf_op jit(solution)/shard_map/ppermute | solution.py:473
  165.8 0.1 collective-permute-start.24
  165.9 2.5 %collective-permute-done.22 = bf16[64,2880]{1,0:T(8,128)(2,1)S(1)} collective-permute-done((bf16[64,2880]{1,0:T(8,128)(2,1)S(1)}, bf16[64,2880]{1,0:T(8,128)(2,1)S(1)}, u32[]{:S(2)}, u32[]{:S(2)}) %collective-permute-start.22) | collective-permute-done | bytes 368672 | tf_op jit(solution)/shard_map/ppermute | solution.py:473
  168.4 0.1 add_convert_fusion.3
  168.5 3.1 %collective-permute-start.23 = (bf16[64,2880]{1,0:T(8,128)(2,1)S(1)}, bf16[64,2880]{1,0:T(8,128)(2,1)S(1)}, u32[]{:S(2)}, u32[]{:S(2)}) collective-permute-start(bf16[64,2880]{1,0:T(8,128)(2,1)S(1)} %add_convert_fusion.3), channel_id=1, source_target_pairs={{0,16},{1,49},{2,18},{3,51},{4,20},{5,53},{6,22},{7,55},{8,24},{9,... | collective-permute-start | bytes 1105928 | tf_op jit(solution)/shard_map/ppermute | solution.py:473
  171.6 6.2 %collective-permute-done.25 = bf16[64,2880]{1,0:T(8,128)(2,1)S(1)} collective-permute-done((bf16[64,2880]{1,0:T(8,128)(2,1)S(1)}, bf16[64,2880]{1,0:T(8,128)(2,1)S(1)}, u32[]{:S(2)}, u32[]{:S(2)}) %collective-permute-start.25) | collective-permute-done | bytes 368672 | tf_op jit(solution)/shard_map/ppermute | solution.py:473
  177.8 0.1 add_convert_fusion.1
  177.9 0.2 collective-permute-start.26
  178.1 2.2 %collective-permute-done.23 = bf16[64,2880]{1,0:T(8,128)(2,1)S(1)} collective-permute-done((bf16[64,2880]{1,0:T(8,128)(2,1)S(1)}, bf16[64,2880]{1,0:T(8,128)(2,1)S(1)}, u32[]{:S(2)}, u32[]{:S(2)}) %collective-permute-start.23) | collective-permute-done | bytes 368672 | tf_op jit(solution)/shard_map/ppermute | solution.py:473
  180.3 0.1 add_convert_fusion.2
  180.5 0.0 copy-start.11
  180.5 5.2 %collective-permute-done.26 = bf16[64,2880]{1,0:T(8,128)(2,1)S(1)} collective-permute-done((bf16[64,2880]{1,0:T(8,128)(2,1)S(1)}, bf16[64,2880]{1,0:T(8,128)(2,1)S(1)}, u32[]{:S(2)}, u32[]{:S(2)}) %collective-permute-start.26) | collective-permute-done | bytes 368672 | tf_op jit(solution)/shard_map/ppermute | solution.py:473
  185.7 0.1 add_convert_fusion
  185.8 0.1 maximum_bitcast_fusion
  185.9 18.8 %all_to_all.30 = bf16[16,8,2880]{2,1,0:T(8,128)(2,1)S(1)} all-to-all(bf16[16,8,2880]{2,1,0:T(8,128)(2,1)S(1)} %maximum_bitcast_fusion), channel_id=1, replica_groups=mesh['ctx'=8,'exp'=16] {'exp'}, dimensions={0} | all-to-all | bytes 1474560 | tf_op jit(solution)/shard_map/all_to_all | solution.py:567
  204.6 1.6 shard_map.135
  (41 shorter events, 0.1 us)
Async XLA Ops:
  0.0 6.1 %copy-start.12 = (s32[128]{0:T(128)S(1)}, s32[128]{0:T(128)}, u32[]{:S(2)}) copy-start(s32[128]{0:T(128)} %param.18) | copy-start | bytes 1540
  0.0 6.1 %copy-start.6 = (bf16[128,4096]{1,0:T(8,128)(2,1)S(1)}, bf16[128,4096]{1,0:T(8,128)(2,1)}, u32[]{:S(2)}) copy-start(bf16[128,4096]{1,0:T(8,128)(2,1)} %q_ref.1) | copy-start | bytes 3145732
  0.0 6.1 %copy-start.8 = (bf16[128,512]{1,0:T(8,128)(2,1)S(1)}, bf16[128,512]{1,0:T(8,128)(2,1)}, u32[]{:S(2)}) copy-start(bf16[128,512]{1,0:T(8,128)(2,1)} %k_ref.1) | copy-start | bytes 393220
  0.0 6.1 %copy-start.9 = (bf16[128,512]{1,0:T(8,128)(2,1)S(1)}, bf16[128,512]{1,0:T(8,128)(2,1)}, u32[]{:S(2)}) copy-start(bf16[128,512]{1,0:T(8,128)(2,1)} %v_ref.1) | copy-start | bytes 393220
  0.0 26.9 %collective-permute-start = (bf16[360,2880]{1,0:T(8,128)(2,1)}, bf16[360,2880]{1,0:T(8,128)(2,1)S(1)}, u32[]{:S(2)}, u32[]{:S(2)}) collective-permute-start(bf16[360,2880]{1,0:T(8,128)(2,1)} %bitcast.22), channel_id=1, source_target_pairs={{0,64},{2,66},{4,68},{6,70},{8,72},{10,74},{12,76},{14,78},{16,80}... | collective-permute-start | bytes 6220808 | tf_op jit(solution)/shard_map/ppermute | solution.py:473
  2.4 32.7 %collective-permute-start.2 = (bf16[1440,512]{1,0:T(8,128)(2,1)S(1)}, bf16[1440,512]{1,0:T(8,128)(2,1)S(1)}, u32[]{:S(2)}, u32[]{:S(2)}) collective-permute-start(bf16[1440,512]{1,0:T(8,128)(2,1)S(1)} %dynamic-slice_bitcast_fusion), channel_id=1, source_target_pairs={{0,66},{1,67},{2,64},{3,65},{4,70},{5,71},{6,68},{7,69},{8,74},{9,... | collective-permute-start | bytes 4423688 | tf_op jit(solution)/shard_map/ppermute | solution.py:473
  6.1 29.0 %copy-start.2 = (bf16[1,2880,360]{1,2,0:T(8,128)(2,1)S(1)}, bf16[1,2880,360]{1,2,0:T(8,128)(2,1)}, u32[]{:S(2)}) copy-start(bf16[1,2880,360]{1,2,0:T(8,128)(2,1)} %param.22) | copy-start | bytes 6220804
  6.3 21.9 %copy-start.1 = (bf16[1,2880,360]{1,2,0:T(8,128)(2,1)S(1)}, bf16[1,2880,360]{1,2,0:T(8,128)(2,1)}, u32[]{:S(2)}) copy-start(bf16[1,2880,360]{1,2,0:T(8,128)(2,1)} %param.21) | copy-start | bytes 6220804
  6.4 36.2 %copy-start.13 = (f32[64]{0:T(128)S(1)}, f32[64]{0:T(128)}, u32[]{:S(2)}) copy-start(f32[64]{0:T(128)} %sinks.3) | copy-start | bytes 772
  26.9 8.2 %collective-permute-start.1 = (bf16[4,144,256]{2,1,0:T(8,128)(2,1)S(1)}, bf16[4,144,256]{2,1,0:T(8,128)(2,1)S(1)}, u32[]{:S(2)}, u32[]{:S(2)}) collective-permute-start(bf16[4,144,256]{2,1,0:T(8,128)(2,1)S(1)} %slice.9), channel_id=1, source_target_pairs={{0,64},{16,80},{32,96},{48,112},{1,65},{17,81},{33,97},{49,113},{2... | collective-permute-start | bytes 884744 | tf_op jit(solution)/shard_map/ppermute | solution.py:536
  28.3 32.3 %collective-permute-start.3 = (bf16[360,2880]{1,0:T(8,128)(2,1)S(1)}, bf16[360,2880]{1,0:T(8,128)(2,1)S(1)}, u32[]{:S(2)}, u32[]{:S(2)}) collective-permute-start(bf16[360,2880]{1,0:T(8,128)(2,1)S(1)} %bitcast.23), channel_id=1, source_target_pairs={{1,17},{3,19},{5,21},{7,23},{9,25},{11,27},{13,29},{15,31},{17,1},... | collective-permute-start | bytes 6220808 | tf_op jit(solution)/shard_map/ppermute | solution.py:473
  35.1 13.2 %copy-start = (bf16[512,2880]{0,1:T(8,128)(2,1)S(1)}, bf16[512,2880]{0,1:T(8,128)(2,1)}, u32[]{:S(2)}) copy-start(bf16[512,2880]{0,1:T(8,128)(2,1)} %param.20) | copy-start | bytes 8847364
  35.1 25.7 %collective-permute-start.4 = (bf16[360,2880]{1,0:T(8,128)(2,1)S(1)}, bf16[360,2880]{1,0:T(8,128)(2,1)S(1)}, u32[]{:S(2)}, u32[]{:S(2)}) collective-permute-start(bf16[360,2880]{1,0:T(8,128)(2,1)S(1)} %bitcast.26), channel_id=1, source_target_pairs={{0,64},{2,66},{4,68},{6,70},{8,72},{10,74},{12,76},{14,78},{16,80}... | collective-permute-start | bytes 6220808 | tf_op jit(solution)/shard_map/ppermute | solution.py:473
  36.1 12.2 %collective-permute-start.5 = (bf16[1440,512]{1,0:T(8,128)(2,1)S(1)}, bf16[1440,512]{1,0:T(8,128)(2,1)S(1)}, u32[]{:S(2)}, u32[]{:S(2)}) collective-permute-start(bf16[1440,512]{1,0:T(8,128)(2,1)S(1)} %collective-permute-done.2.w_first), channel_id=1, source_target_pairs={{0,1},{1,0},{2,3},{3,2},{4,5},{5,4},{6,7},{7,6},{8,9},{9,8},{10,11... | collective-permute-start | bytes 4423688 | tf_op jit(solution)/shard_map/ppermute | solution.py:473
  48.3 5.5 %copy-start.3 = (bf16[1,360,2880]{2,1,0:T(8,128)(2,1)S(1)}, bf16[1,360,2880]{2,1,0:T(8,128)(2,1)}, u32[]{:S(2)}) copy-start(bf16[1,360,2880]{2,1,0:T(8,128)(2,1)} %param.23) | copy-start | bytes 6220804
  50.1 12.6 %collective-permute-start.6 = (bf16[1440,128]{1,0:T(8,128)(2,1)S(1)}, bf16[1440,128]{1,0:T(8,128)(2,1)S(1)}, u32[]{:S(2)}, u32[]{:S(2)}) collective-permute-start(bf16[1440,128]{1,0:T(8,128)(2,1)S(1)} %get-tuple-element.59), channel_id=1, source_target_pairs={{0,16},{16,32},{32,48},{48,0},{64,80},{80,96},{96,112},{112,64},{1... | collective-permute-start | bytes 1105928 | tf_op jit(solution)/shard_map/ppermute | solution.py:41
  52.6 10.6 %collective-permute-start.7 = (bf16[1440,128]{1,0:T(8,128)(2,1)S(1)}, bf16[1440,128]{1,0:T(8,128)(2,1)S(1)}, u32[]{:S(2)}, u32[]{:S(2)}) collective-permute-start(bf16[1440,128]{1,0:T(8,128)(2,1)S(1)} %get-tuple-element.60), channel_id=1, source_target_pairs={{0,48},{16,0},{32,16},{48,32},{64,112},{80,64},{96,80},{112,96},{1... | collective-permute-start | bytes 1105928 | tf_op jit(solution)/shard_map/ppermute | solution.py:45
  53.8 31.3 %collective-permute-start.12 = (bf16[360,2880]{1,0:T(8,128)(2,1)S(1)}, bf16[360,2880]{1,0:T(8,128)(2,1)S(1)}, u32[]{:S(2)}, u32[]{:S(2)}) collective-permute-start(bf16[360,2880]{1,0:T(8,128)(2,1)S(1)} %bitcast.30), channel_id=1, source_target_pairs={{0,64},{2,66},{4,68},{6,70},{8,72},{10,74},{12,76},{14,78},{16,80}... | collective-permute-start | bytes 6220808 | tf_op jit(solution)/shard_map/ppermute | solution.py:473
  60.6 8.1 %collective-permute-start.9 = (bf16[1440,128]{1,0:T(8,128)(2,1)S(1)}, bf16[1440,128]{1,0:T(8,128)(2,1)S(1)}, u32[]{:S(2)}, u32[]{:S(2)}) collective-permute-start(bf16[1440,128]{1,0:T(8,128)(2,1)S(1)} %get-tuple-element.64), channel_id=1, source_target_pairs={{0,16},{16,32},{32,48},{48,0},{64,80},{80,96},{96,112},{112,64},{1... | collective-permute-start | bytes 1105928 | tf_op jit(solution)/shard_map/ppermute | solution.py:41
  63.2 20.7 %copy-start.14 = (f32[2880]{0:T(1024)S(1)}, f32[2880]{0:T(1024)}, u32[]{:S(2)}) copy-start(f32[2880]{0:T(1024)} %param.19) | copy-start | bytes 34564
  63.2 20.7 %copy-start.7 = (bf16[128,2880]{0,1:T(8,128)(2,1)S(1)}, bf16[128,2880]{0,1:T(8,128)(2,1)}, u32[]{:S(2)}) copy-start(bf16[128,2880]{0,1:T(8,128)(2,1)} %param.13) | copy-start | bytes 2211844
  63.2 20.7 %copy-start.10 = (s32[128,4]{0,1:T(4,128)S(1)}, s32[128,4]{0,1:T(4,128)}, u32[]{:S(2)}) copy-start(s32[128,4]{0,1:T(4,128)} %param.24) | copy-start | bytes 6148
  65.2 6.7 %collective-permute-start.10 = (bf16[1440,128]{1,0:T(8,128)(2,1)S(1)}, bf16[1440,128]{1,0:T(8,128)(2,1)S(1)}, u32[]{:S(2)}, u32[]{:S(2)}) collective-permute-start(bf16[1440,128]{1,0:T(8,128)(2,1)S(1)} %get-tuple-element.65), channel_id=1, source_target_pairs={{0,48},{16,0},{32,16},{48,32},{64,112},{80,64},{96,80},{112,96},{1... | collective-permute-start | bytes 1105928 | tf_op jit(solution)/shard_map/ppermute | solution.py:45
  67.2 11.4 %collective-permute-start.11 = (bf16[1440,128]{1,0:T(8,128)(2,1)S(1)}, bf16[1440,128]{1,0:T(8,128)(2,1)S(1)}, u32[]{:S(2)}, u32[]{:S(2)}) collective-permute-start(bf16[1440,128]{1,0:T(8,128)(2,1)S(1)} %get-tuple-element.66), channel_id=1, source_target_pairs={{0,48},{16,0},{32,16},{48,32},{64,112},{80,64},{96,80},{112,96},{1... | collective-permute-start | bytes 1105928 | tf_op jit(solution)/shard_map/ppermute | solution.py:45
  67.3 11.3 %collective-permute-start.8 = (bf16[1440,128]{1,0:T(8,128)(2,1)S(1)}, bf16[1440,128]{1,0:T(8,128)(2,1)S(1)}, u32[]{:S(2)}, u32[]{:S(2)}) collective-permute-start(bf16[1440,128]{1,0:T(8,128)(2,1)S(1)} %get-tuple-element.63), channel_id=1, source_target_pairs={{0,16},{16,32},{32,48},{48,0},{64,80},{80,96},{96,112},{112,64},{1... | collective-permute-start | bytes 1105928 | tf_op jit(solution)/shard_map/ppermute | solution.py:41
  78.6 33.7 %collective-permute-start.13 = (bf16[360,2880]{1,0:T(8,128)(2,1)S(1)}, bf16[360,2880]{1,0:T(8,128)(2,1)S(1)}, u32[]{:S(2)}, u32[]{:S(2)}) collective-permute-start(bf16[360,2880]{1,0:T(8,128)(2,1)S(1)} %bitcast.27), channel_id=1, source_target_pairs={{1,17},{3,19},{5,21},{7,23},{9,25},{11,27},{13,29},{15,31},{17,1},... | collective-permute-start | bytes 6220808 | tf_op jit(solution)/shard_map/ppermute | solution.py:473
  81.4 57.7 %collective-permute-start.20 = (bf16[360,2880]{1,0:T(8,128)(2,1)S(1)}, bf16[360,2880]{1,0:T(8,128)(2,1)S(1)}, u32[]{:S(2)}, u32[]{:S(2)}) collective-permute-start(bf16[360,2880]{1,0:T(8,128)(2,1)S(1)} %bitcast.31), channel_id=1, source_target_pairs={{1,17},{3,19},{5,21},{7,23},{9,25},{11,27},{13,29},{15,31},{17,1},... | collective-permute-start | bytes 6220808 | tf_op jit(solution)/shard_map/ppermute | solution.py:473
  112.3 11.3 %collective-permute-start.14 = (bf16[64,2880]{1,0:T(8,128)(2,1)S(1)}, bf16[64,2880]{1,0:T(8,128)(2,1)S(1)}, u32[]{:S(2)}, u32[]{:S(2)}) collective-permute-start(bf16[64,2880]{1,0:T(8,128)(2,1)S(1)} %get-tuple-element.100.refs_0_), channel_id=1, source_target_pairs={{0,16},{1,49},{2,18},{3,51},{4,20},{5,53},{6,22},{7,55},{8,24},{9,... | collective-permute-start | bytes 1105928 | tf_op jit(solution)/shard_map/ppermute | solution.py:473
  116.5 12.1 %collective-permute-start.16 = (bf16[64,2880]{1,0:T(8,128)(2,1)S(1)}, bf16[64,2880]{1,0:T(8,128)(2,1)S(1)}, u32[]{:S(2)}, u32[]{:S(2)}) collective-permute-start(bf16[64,2880]{1,0:T(8,128)(2,1)S(1)} %get-tuple-element.99.refs_1_), channel_id=1, source_target_pairs={{16,0},{49,1},{18,2},{51,3},{20,4},{53,5},{22,6},{55,7},{24,8},{57... | collective-permute-start | bytes 1105928 | tf_op jit(solution)/shard_map/ppermute | solution.py:473
  116.5 22.6 %collective-permute-start.18 = (bf16[64,2880]{1,0:T(8,128)(2,1)S(1)}, bf16[64,2880]{1,0:T(8,128)(2,1)S(1)}, u32[]{:S(2)}, u32[]{:S(2)}) collective-permute-start(bf16[64,2880]{1,0:T(8,128)(2,1)S(1)} %get-tuple-element.99.refs_1_), channel_id=1, source_target_pairs={{0,16},{1,49},{2,18},{3,51},{4,20},{5,53},{6,22},{7,55},{8,24},{9,... | collective-permute-start | bytes 1105928 | tf_op jit(solution)/shard_map/ppermute | solution.py:473
  119.2 19.9 %collective-permute-start.19 = (bf16[64,2880]{1,0:T(8,128)(2,1)S(1)}, bf16[64,2880]{1,0:T(8,128)(2,1)S(1)}, u32[]{:S(2)}, u32[]{:S(2)}) collective-permute-start(bf16[64,2880]{1,0:T(8,128)(2,1)S(1)} %get-tuple-element.100.refs_0_), channel_id=1, source_target_pairs={{16,0},{49,1},{18,2},{51,3},{20,4},{53,5},{22,6},{55,7},{24,8},{57... | collective-permute-start | bytes 1105928 | tf_op jit(solution)/shard_map/ppermute | solution.py:473
  123.6 26.7 %collective-permute-start.15 = (bf16[64,2880]{1,0:T(8,128)(2,1)S(1)}, bf16[64,2880]{1,0:T(8,128)(2,1)S(1)}, u32[]{:S(2)}, u32[]{:S(2)}) collective-permute-start(bf16[64,2880]{1,0:T(8,128)(2,1)S(1)} %collective-permute-done.14.refs_2_), channel_id=1, source_target_pairs={{0,16},{1,49},{2,18},{3,51},{4,20},{5,53},{6,22},{7,55},{8,24},{9,... | collective-permute-start | bytes 1105928 | tf_op jit(solution)/shard_map/ppermute | solution.py:473
  128.5 21.7 %collective-permute-start.17 = (bf16[64,2880]{1,0:T(8,128)(2,1)S(1)}, bf16[64,2880]{1,0:T(8,128)(2,1)S(1)}, u32[]{:S(2)}, u32[]{:S(2)}) collective-permute-start(bf16[64,2880]{1,0:T(8,128)(2,1)S(1)} %collective-permute-done.16.refs_5_), channel_id=1, source_target_pairs={{16,0},{49,1},{18,2},{51,3},{20,4},{53,5},{22,6},{55,7},{24,8},{57... | collective-permute-start | bytes 1105928 | tf_op jit(solution)/shard_map/ppermute | solution.py:473
  139.1 1.3 copy-start.4
  150.3 1.6 copy-start.5
  157.1 11.3 %collective-permute-start.22 = (bf16[64,2880]{1,0:T(8,128)(2,1)S(1)}, bf16[64,2880]{1,0:T(8,128)(2,1)S(1)}, u32[]{:S(2)}, u32[]{:S(2)}) collective-permute-start(bf16[64,2880]{1,0:T(8,128)(2,1)S(1)} %get-tuple-element.94), channel_id=1, source_target_pairs={{0,16},{1,49},{2,18},{3,51},{4,20},{5,53},{6,22},{7,55},{8,24},{9,... | collective-permute-start | bytes 1105928 | tf_op jit(solution)/shard_map/ppermute | solution.py:473
  159.4 18.7 %collective-permute-start.21 = (bf16[64,2880]{1,0:T(8,128)(2,1)S(1)}, bf16[64,2880]{1,0:T(8,128)(2,1)S(1)}, u32[]{:S(2)}, u32[]{:S(2)}) collective-permute-start(bf16[64,2880]{1,0:T(8,128)(2,1)S(1)} %get-tuple-element.90), channel_id=1, source_target_pairs={{16,0},{49,1},{18,2},{51,3},{20,4},{53,5},{22,6},{55,7},{24,8},{57... | collective-permute-start | bytes 1105928 | tf_op jit(solution)/shard_map/ppermute | solution.py:473
  163.2 14.6 %collective-permute-start.25 = (bf16[64,2880]{1,0:T(8,128)(2,1)S(1)}, bf16[64,2880]{1,0:T(8,128)(2,1)S(1)}, u32[]{:S(2)}, u32[]{:S(2)}) collective-permute-start(bf16[64,2880]{1,0:T(8,128)(2,1)S(1)} %get-tuple-element.98), channel_id=1, source_target_pairs={{16,0},{49,1},{18,2},{51,3},{20,4},{53,5},{22,6},{55,7},{24,8},{57... | collective-permute-start | bytes 1105928 | tf_op jit(solution)/shard_map/ppermute | solution.py:473
  165.8 14.7 %collective-permute-start.24 = (bf16[64,2880]{1,0:T(8,128)(2,1)S(1)}, bf16[64,2880]{1,0:T(8,128)(2,1)S(1)}, u32[]{:S(2)}, u32[]{:S(2)}) collective-permute-start(bf16[64,2880]{1,0:T(8,128)(2,1)S(1)} %get-tuple-element.96), channel_id=1, source_target_pairs={{0,16},{1,49},{2,18},{3,51},{4,20},{5,53},{6,22},{7,55},{8,24},{9,... | collective-permute-start | bytes 1105928 | tf_op jit(solution)/shard_map/ppermute | solution.py:473
  168.5 11.8 %collective-permute-start.23 = (bf16[64,2880]{1,0:T(8,128)(2,1)S(1)}, bf16[64,2880]{1,0:T(8,128)(2,1)S(1)}, u32[]{:S(2)}, u32[]{:S(2)}) collective-permute-start(bf16[64,2880]{1,0:T(8,128)(2,1)S(1)} %add_convert_fusion.3), channel_id=1, source_target_pairs={{0,16},{1,49},{2,18},{3,51},{4,20},{5,53},{6,22},{7,55},{8,24},{9,... | collective-permute-start | bytes 1105928 | tf_op jit(solution)/shard_map/ppermute | solution.py:473
  177.9 7.7 %collective-permute-start.26 = (bf16[64,2880]{1,0:T(8,128)(2,1)S(1)}, bf16[64,2880]{1,0:T(8,128)(2,1)S(1)}, u32[]{:S(2)}, u32[]{:S(2)}) collective-permute-start(bf16[64,2880]{1,0:T(8,128)(2,1)S(1)} %add_convert_fusion.1), channel_id=1, source_target_pairs={{16,0},{49,1},{18,2},{51,3},{20,4},{53,5},{22,6},{55,7},{24,8},{57... | collective-permute-start | bytes 1105928 | tf_op jit(solution)/shard_map/ppermute | solution.py:473
  180.5 24.2 %copy-start.11 = (f32[128,4]{0,1:T(4,128)S(1)}, f32[128,4]{0,1:T(4,128)}, u32[]{:S(2)}) copy-start(f32[128,4]{0,1:T(4,128)} %param.25) | copy-start | bytes 6148

commit v2 on v1

--- a/solution.py
+++ b/solution.py
@@ -357,91 +357,95 @@
     )(hidden, back, ids, weights)
 
 
-LOADS = ((2, 3), (4, 5), (7, 8))
-
-
-def expert_kernel(sizes, *refs):
+def expert_kernel(sizes, plan, count_out, compute, *refs):
     count = len(sizes)
-    pieces, weights, outs = refs[:count], refs[count : count + 9], refs[count + 9 : 2 * count + 9]
-    rows_x, held, sem = refs[2 * count + 9], refs[2 * count + 10 : 2 * count + 13], refs[-1]
+    total = max(max(group) for group in plan) + 1
+    pieces, weights = refs[:count], refs[count : count + total]
+    outs = refs[count + total : count + total + count_out]
+    rows, held, sem = refs[count + total + count_out], refs[count + total + count_out + 1 : -1], refs[-1]
     core = lax.rem(lax.axis_index("exp"), 2)
+
+    def load(index, act):
+        group = plan[index]
+        for which, source in enumerate(group):
+
+            def go(source=source):
+                act(pltpu.make_async_copy(weights[source], held[index], sem.at[count + index]))
+
+            if len(group) == 1:
+                go()
+            else:
+                pl.when(core == which)(go)
+
     copies = []
     start = 0
     for index, (piece, size) in enumerate(zip(pieces, sizes)):
-        copies.append(
-            pltpu.make_async_copy(piece, rows_x.at[pl.ds(start, size)], sem.at[index])
-        )
+        copies.append(pltpu.make_async_copy(piece, rows.at[pl.ds(start, size)], sem.at[index]))
         start += size
-    loads = []
-    for index, (group, dst) in enumerate(zip(LOADS, held)):
-        loads.append(
-            [pltpu.make_async_copy(weights[w], dst, sem.at[count + index]) for w in group]
-        )
-
-    def each(load, act):
-        for which, copy in enumerate(load):
-
-            @pl.when(core == which)
-            def _(copy=copy):
-                act(copy)
-
-    def start_load(load):
-        each(load, lambda copy: copy.start())
-
-    def wait_load(load):
-        each(load, lambda copy: copy.wait())
-
     for copy in copies:
         copy.start()
-    for load in loads:
-        start_load(load)
+    for index in range(len(plan)):
+        load(index, lambda copy: copy.start())
     for copy in copies:
         copy.wait()
-    x = rows_x[...]
-    gate_own, up_own, down_own = weights[0], weights[1], weights[6]
-    gate_near, up_near, down_near = held
-
-    def hidden_units(gate, up, ready):
-        g = lax.dot_general(x, gate[...], NT, preferred_element_type=jnp.float32)
-        ready()
-        v = lax.dot_general(x, up[...], NT, preferred_element_type=jnp.float32)
-        return ((v + 1.0) * g * jax.nn.sigmoid(1.702 * g)).astype(jnp.bfloat16)
-
-    act_own = hidden_units(gate_own, up_own, lambda: None)
-    wait_load(loads[0])
-    act_near = hidden_units(gate_near, up_near, lambda: wait_load(loads[1]))
-    wait_load(loads[2])
+
+    def weight(index):
+        load(index, lambda copy: copy.wait())
+        return held[index]
+
+    compute(rows, weight, outs)
+
+
+def expert_call(pieces, weights, plan, outs, compute, flops):
+    sizes = tuple(piece.shape[0] for piece in pieces)
+    return pl.pallas_call(
+        functools.partial(expert_kernel, sizes, plan, len(outs), compute),
+        out_shape=tuple(jax.ShapeDtypeStruct(shape, jnp.bfloat16) for shape in outs),
+        in_specs=[spec(ANY)] * (len(sizes) + len(weights)),
+        out_specs=tuple(spec(VMEM) for _ in outs),
+        scratch_shapes=[pltpu.VMEM((sum(sizes), pieces[0].shape[1]), jnp.bfloat16)]
+        + [pltpu.VMEM((FFS, D), jnp.bfloat16)] * len(plan)
+        + [pltpu.SemaphoreType.DMA((len(sizes) + len(plan),))],
+        compiler_params=params(24),
+        cost_estimate=pl.CostEstimate(flops=flops, bytes_accessed=4 << 20, transcendentals=0),
+    )(*pieces, *weights)
+
+
+def act_compute(rows, weight, outs):
+    x = rows[...]
+    for part, out in enumerate(outs):
+        g = lax.dot_general(x, weight(2 * part)[...], NT, preferred_element_type=jnp.float32)
+        v = lax.dot_general(x, weight(2 * part + 1)[...], NT, preferred_element_type=jnp.float32)
+        out[...] = ((v + 1.0) * g * jax.nn.sigmoid(1.702 * g)).astype(jnp.bfloat16)
+
+
+def hidden_units(pieces, weights):
+    rows = sum(piece.shape[0] for piece in pieces)
+    return expert_call(
+        pieces, weights, ((0,), (1,), (2, 3), (4, 5)), [(rows, FFS)] * 2, act_compute, 8 * rows * D * FFS
+    )
+
+
+def down_compute(rows, weight, outs):
+    half = rows.shape[0] // 2
+    own, near = rows[0:half], rows[half:]
+    down_own, down_near = weight(0), weight(1)
     for first in range(0, D, 512):
         cols = slice(first, min(first + 512, D))
-        part = jnp.dot(act_own, down_own[:, cols], preferred_element_type=jnp.float32)
-        part = part + jnp.dot(act_near, down_near[:, cols], preferred_element_type=jnp.float32)
+        part = jnp.dot(own, down_own[:, cols], preferred_element_type=jnp.float32)
+        part = part + jnp.dot(near, down_near[:, cols], preferred_element_type=jnp.float32)
         part = part.astype(jnp.bfloat16)
         start = 0
-        for out, size in zip(outs, sizes):
-            out[:, cols] = part[start : start + size]
-            start += size
-
-
-def experts(pieces, weights):
-    sizes = tuple(piece.shape[0] for piece in pieces)
-    total = sum(sizes)
-    return pl.pallas_call(
-        functools.partial(expert_kernel, sizes),
-        out_shape=tuple(jax.ShapeDtypeStruct((size, D), jnp.bfloat16) for size in sizes),
-        in_specs=[spec(ANY)] * len(sizes)
-        + [spec(VMEM)] * 2
-        + [spec(ANY)] * 4
-        + [spec(VMEM)]
-        + [spec(ANY)] * 2,
-        out_specs=tuple(spec(VMEM) for _ in sizes),
-        scratch_shapes=[pltpu.VMEM((total, D), jnp.bfloat16)]
-        + [pltpu.VMEM((FFS, D), jnp.bfloat16)] * 3
-        + [pltpu.SemaphoreType.DMA((len(sizes) + 3,))],
-        compiler_params=params(32),
-        cost_estimate=pl.CostEstimate(
-            flops=12 * total * D * FFS, bytes_accessed=14 << 20, transcendentals=2 * total * FFS
-        ),
-    )(*pieces, *weights)
+        for out in outs:
+            out[:, cols] = part[start : start + out.shape[0]]
+            start += out.shape[0]
+
+
+def from_hidden(acts, weights):
+    rows = acts[0].shape[0]
+    return expert_call(
+        acts, weights, ((0,), (1, 2)), [(rows // 4, D)] * 4, down_compute, 4 * rows * D * FFS
+    )
 
 
 def over_all(move):
@@ -464,8 +468,8 @@
     return (y, 3 - x, z, hi, core) if across else (1 - y, x, z, hi, core)
 
 
-def across_y(y, x, z, hi, core):
-    place = (2 * hi + y + (1 if y == 1 else 3)) % 4
+def beside(y, x, z, hi, core):
+    place = (2 * hi + y + (3 if core == 0 else 1)) % 4
     return place % 2, x, z, place // 2, core
 
 
@@ -475,28 +479,32 @@
 
 NEXT = over_all(onward)
 BACK = [(b, a) for a, b in NEXT]
-PARTNER = [[(a, b) for a, b in over_all(partner) if a % 2 == core] for core in range(2)]
-ACROSS = over_all(across_y)
+PARTNER = over_all(partner)
+PARTNER_0 = [(a, b) for a, b in PARTNER if a % 2 == 0]
+PARTNER_1 = [(a, b) for a, b in PARTNER if a % 2 == 1]
+BESIDE = over_all(beside)
 SWAP = over_all(lambda y, x, z, hi, core: (y, x, z, hi, 1 - core))
 
 
-def exchange_experts(arrived, weights):
+def exchange_experts(arrived, into, out_of):
     half = TOK // 2
     own_a, own_b = arrived[:half], arrived[half:]
     prev_a, next_b = permute(own_a, NEXT), permute(own_b, BACK)
     prev_b, next_a = permute(own_b, NEXT), permute(own_a, BACK)
     opp_a, opp_b = permute(prev_a, NEXT), permute(next_b, BACK)
-    oo_a, oo_b, op_a, op_b, on_a, on_b = experts(
-        (own_a, own_b, prev_a, prev_b, next_a, next_b), weights
-    )
-    opp_a, opp_b, oo_a, oo_b, op_a, op_b, on_a, on_b = lax.optimization_barrier(
-        (opp_a, opp_b, oo_a, oo_b, op_a, op_b, on_a, on_b)
-    )
-    far_a, far_b = experts((opp_a, opp_b), weights)
-    on_at_next, op_at_prev = permute(far_a, NEXT), permute(far_b, BACK)
+    acts = hidden_units((own_a, own_b, prev_a, next_b), into)
+    opp_a, opp_b, prev_b, next_a, acts = lax.optimization_barrier(
+        (opp_a, opp_b, prev_b, next_a, acts)
+    )
+    oo_a, oo_b, op_a, on_b = from_hidden(acts, out_of)
     got_b, got_a = permute(on_b, NEXT), permute(op_a, BACK)
-    more_a = permute(add(on_a, on_at_next), NEXT)
-    more_b = permute(add(op_b, op_at_prev), BACK)
+    acts = hidden_units((opp_a, opp_b, prev_b, next_a), into)
+    far_a, far_b, op_b, on_a = from_hidden(acts, out_of)
+    got_a, got_b, far_a, far_b, op_b, on_a = lax.optimization_barrier(
+        (got_a, got_b, far_a, far_b, op_b, on_a)
+    )
+    more_a = permute(add(on_a, permute(far_a, NEXT)), NEXT)
+    more_b = permute(add(op_b, permute(far_b, BACK)), BACK)
     return jnp.concatenate([add(oo_a, got_a, more_a), add(oo_b, got_b, more_b)], axis=0)
 
 
@@ -520,8 +528,7 @@
     w_own = out_weight.T
 
     mine = lax.dynamic_slice_in_dim(w_own, core * (D // 2), D // 2, 0)
-    w_first = permute(mine, ACROSS)
-    gate_0 = permute(gate, PARTNER[0])
+    w_first = permute(mine, BESIDE)
 
     packed = pack(queries, keys, values, segments)
     packed = lax.all_to_all(
@@ -532,18 +539,21 @@
         tiled=True,
         axis_index_groups=[[0, 1, 2, 3], [4, 5, 6, 7]],
     )
-    packed, gate_0, gate_out = lax.optimization_barrier((packed, gate_0, gate))
+    packed, w_first, gate_out = lax.optimization_barrier((packed, w_first, gate))
     low = lax.ppermute(packed[:, :, 1024:], "ctx", [(x, x + 4) for x in range(4)])
-    gate_1 = permute(gate_out, PARTNER[1])
-    low, w_first, up_out, down_out = lax.optimization_barrier((low, w_first, up, down))
+    gate_1 = permute(gate_out, PARTNER_1)
     w_second = permute(w_first, SWAP)
-    up_0, down_0 = permute(up_out, PARTNER[0]), permute(down_out, PARTNER[0])
+    low, gate_out = lax.optimization_barrier((low, gate))
+    gate_0 = permute(gate_out, PARTNER_0)
 
     attn = attend((2, 1), sinks, packed, low)
     opp_a, opp_b, plus_a, plus_b = project(attn, w_own, w_first, w_second)
     ra, lb, right_b = go_right(opp_a), go_left(opp_b), go_right(plus_b)
     attn = attend((3, 0), sinks, packed, low)
-    attn, gate_1, up_0 = lax.optimization_barrier((attn, gate_1, up_0))
+    attn, ra, lb, right_b, gate_0, gate_1, up_out, down_out = lax.optimization_barrier(
+        (attn, ra, lb, right_b, gate_0, gate_1, up, down)
+    )
+    up_0, down_0 = permute(up_out, PARTNER_0), permute(down_out, PARTNER_0)
     to_right, to_left_a, to_left_b, own_a, own_b = project(
         attn, w_own, w_first, w_second, plus_a, ra, lb
     )
@@ -552,17 +562,17 @@
     right_a, right_b, left_a, left_b, up_out, down_out = lax.optimization_barrier(
         (right_a, right_b, left_a, left_b, up, down)
     )
-    up_1, down_1 = permute(up_out, PARTNER[1]), permute(down_out, PARTNER[1])
+    up_1, down_1 = permute(up_out, PARTNER_1), permute(down_out, PARTNER_1)
 
     ids = expert_ids.T
     hidden, send = norm(
         resid_in.T, own_a, own_b, right_a, right_b, left_a, left_b, norm_gain.reshape(1, D), ids
     )
-    send, down_0 = lax.optimization_barrier((send, down_0))
+    send, up_0 = lax.optimization_barrier((send, up_0))
     arrived = lax.all_to_all(send, "exp", split_axis=0, concat_axis=0, tiled=True)
-    arrived, up_1 = lax.optimization_barrier((arrived, up_1))
+    arrived, down_0 = lax.optimization_barrier((arrived, down_0))
     summed = exchange_experts(
-        arrived, (gate, up, gate_0, gate_1, up_0, up_1, down, down_0, down_1)
+        arrived, (gate, up, gate_0, gate_1, up_0, up_1), (down, down_0, down_1)
     )
     back = lax.all_to_all(summed, "exp", split_axis=0, concat_axis=0, tiled=True)
     return combine(hidden, back, ids, route_weights.T).T

time: 208 us -> 225 us (1.082)
  waiting for transfers between devices: 49.5 us -> 72.2 us
  blocking collectives: 66.4 us -> 51.3 us
  local copies, waits for them, and re-layouts: 4.54 us -> 10.6 us
  Pallas kernels: 33.4 us -> 38.9 us
    all_to_all x1 -> x0, blocking collectives: 27.1 us -> none  [on_device(): lax.all_to_all(send, 'exp', split_axis=0, concat_axis=0, tiled=True)]
    all_to_all x0 -> x1, waiting for transfers between devices: none -> 20 us  [on_device(): lax.all_to_all(send, 'exp', split_axis=0, concat_axis=0, tiled=True)]
    ppermute x20, waiting for transfers between devices: 37.2 us -> 22.8 us  [permute(): return lax.ppermute(v, ('ctx', 'exp'), pairs)]
    ppermute x3, waiting for transfers between devices: 1.81 us -> 16.1 us  [go_right(): return lax.ppermute(v, 'ctx', RIGHT)]
    ppermute x20, starting transfers between devices: 42.6 us -> 30.5 us  [permute(): return lax.ppermute(v, ('ctx', 'exp'), pairs)]
    all_to_all x1, blocking collectives: 18.8 us -> 30.3 us  [on_device(): lax.all_to_all(summed, 'exp', split_axis=0, concat_axis=0, tiled=True)]
    unnamed x30 -> x48, local copies, waits for them, and re-layouts: 2.98 us -> 8.99 us
    all_to_all x0 -> x1, starting transfers between devices: none -> 5.43 us  [on_device(): lax.all_to_all(send, 'exp', split_axis=0, concat_axis=0, tiled=True)]
  transfers between devices with their start and end apart: 27 -> 28, of which waited for: 12 -> 14; matrix products, arithmetic and copies ran while one was open for 1% -> 0% of each run, Pallas kernels for 13% -> 15%
where the time goes in v2:
time: 225 us; the launch traced here: 224 us
  waiting for transfers between devices  72.2 us (32%)
  blocking collectives  51.3 us (23%)
  starting transfers between devices  50.2 us (22%)
  Pallas kernels  38.9 us (17%)
  local copies, waits for them, and re-layouts  10.6 us (5%)
    ppermute x20, starting transfers between devices, permute(): return lax.ppermute(v, ('ctx', 'exp'), pairs)  30.5 us
    all_to_all x1, blocking collectives, on_device(): lax.all_to_all(summed, 'exp', split_axis=0, concat_axis=0, tiled=True)  30.3 us
    ppermute x20, waiting for transfers between devices, permute(): return lax.ppermute(v, ('ctx', 'exp'), pairs)  22.8 us
    all_to_all x1, blocking collectives, on_device(): lax.all_to_all(packed, 'ctx', split_axis=0, concat_axis=0, tiled=True, ax...  21 us
    all_to_all x1, waiting for transfers between devices, on_device(): lax.all_to_all(send, 'exp', split_axis=0, concat_axis=0, tiled=True)  20 us
    pallas_call x4, Pallas kernels, expert_call(): pl.pallas_call(functools.partial(expert_kernel, sizes, plan, len(outs), c...  19.5 us
    ppermute x3, waiting for transfers between devices, go_right(): return lax.ppermute(v, 'ctx', RIGHT)  16.1 us
    pallas_call x2, Pallas kernels, attend(): pl.pallas_call(functools.partial(attend_kernel, steps), out_shape=jax.Sha...  11.8 us
  transfers between devices with their start and end apart: 28, of which 14 were waited for; matrix products, arithmetic and copies ran while one was open for 0% of the time, Pallas kernels for 15%

profile of v2, /device:TPU:1, one launch (start us, length us, event | category | flops | bytes accessed | tf_op | source)
XLA Modules:
  0.0 224.1 jit_solution(1092259429341224270)
XLA Ops:
  0.0 1.6 dynamic-slice_bitcast_fusion
  1.6 2.2 collective-permute-start
  3.8 0.2 shard_map.127
  4.1 21.0 %all_to_all.28.pack_ref = bf16[4,144,1280]{2,1,0:T(8,128)(2,1)S(1)} all-to-all(bf16[4,144,1280]{2,1,0:T(8,128)(2,1)S(1)} %shard_map.127), channel_id=1, replica_groups={{0,16,32,48},{64,80,96,112},{1,17,33,49},{65,81,97,113},{2,18,34,50},{6..., dimensions={0} | all-to-all | bytes 2949120 | tf_op jit(solution)/shard_map/all_to_all | solution.py:534
  25.1 6.2 %collective-permute-start.1 = (bf16[4,144,256]{2,1,0:T(8,128)(2,1)S(1)}, bf16[4,144,256]{2,1,0:T(8,128)(2,1)S(1)}, u32[]{:S(2)}, u32[]{:S(2)}) collective-permute-start(bf16[4,144,256]{2,1,0:T(8,128)(2,1)S(1)} %slice.9), channel_id=1, source_target_pairs={{0,64},{16,80},{32,96},{48,112},{1,65},{17,81},{33,97},{49,113},{2... | collective-permute-start | bytes 884744 | tf_op jit(solution)/shard_map/ppermute | solution.py:543
  31.3 2.2 collective-permute-start.7
  33.5 3.2 %collective-permute-done.1.low_ref = bf16[4,144,256]{2,1,0:T(8,128)(2,1)S(1)} collective-permute-done((bf16[4,144,256]{2,1,0:T(8,128)(2,1)S(1)}, bf16[4,144,256]{2,1,0:T(8,128)(2,1)S(1)}, u32[]{:S(2)}, u32[]{:S(2)}) %collective-permute-start.1) | collective-permute-done | bytes 294944 | tf_op jit(solution)/shard_map/ppermute | solution.py:543
  36.7 0.8 collective-permute-start.6
  37.5 5.4 %collective-permute-start.2 = (bf16[1440,512]{1,0:T(8,128)(2,1)S(1)}, bf16[1440,512]{1,0:T(8,128)(2,1)S(1)}, u32[]{:S(2)}, u32[]{:S(2)}) collective-permute-start(bf16[1440,512]{1,0:T(8,128)(2,1)S(1)} %collective-permute-done.w_first), channel_id=1, source_target_pairs={{0,1},{1,0},{2,3},{3,2},{4,5},{5,4},{6,7},{7,6},{8,9},{9,8},{10,11... | collective-permute-start | bytes 4423688 | tf_op jit(solution)/shard_map/ppermute | solution.py:477
  43.0 5.8 %shard_map.129.attn = bf16[256,1024]{1,0:T(8,128)(2,1)S(1)} custom-call(f32[64]{0:T(128)S(1)} %copy-done.22, bf16[4,144,1280]{2,1,0:T(8,128)(2,1)S(1)} %all_to_all.28.pack_ref, bf16[4,144,256]{2,1,0:T(8,128)(2,1)S(1)} %collective-permute-done.1.low_ref), custom_call_target="tpu_custom_call" | custom-call | flops 2147483648 | bytes 4194304 | tf_op jit(solution)/shard_map/pallas_call | solution.py:205
  48.8 1.8 shard_map.130
  50.6 0.8 collective-permute-start.3
  51.4 1.9 collective-permute-start.4
  53.3 6.0 %shard_map.128.attn = bf16[256,1024]{1,0:T(8,128)(2,1)S(1)} custom-call(f32[64]{0:T(128)S(1)} %copy-done.22, bf16[4,144,1280]{2,1,0:T(8,128)(2,1)S(1)} %all_to_all.28.pack_ref, bf16[4,144,256]{2,1,0:T(8,128)(2,1)S(1)} %collective-permute-done.1.low_ref), custom_call_target="tpu_custom_call" | custom-call | flops 2147483648 | bytes 4194304 | tf_op jit(solution)/shard_map/pallas_call | solution.py:205
  59.3 9.3 %collective-permute-done.3.refs_1_ = bf16[1440,128]{1,0:T(8,128)(2,1)S(1)} collective-permute-done((bf16[1440,128]{1,0:T(8,128)(2,1)S(1)}, bf16[1440,128]{1,0:T(8,128)(2,1)S(1)}, u32[]{:S(2)}, u32[]{:S(2)}) %collective-permute-start.3) | collective-permute-done | bytes 368672 | tf_op jit(solution)/shard_map/ppermute | solution.py:41
  68.6 3.9 %collective-permute-done.5.left_b = bf16[1440,128]{1,0:T(8,128)(2,1)S(1)} collective-permute-done((bf16[1440,128]{1,0:T(8,128)(2,1)S(1)}, bf16[1440,128]{1,0:T(8,128)(2,1)S(1)}, u32[]{:S(2)}, u32[]{:S(2)}) %collective-permute-start.5) | collective-permute-done | bytes 368672 | tf_op jit(solution)/shard_map/ppermute | solution.py:41
  72.5 0.8 collective-permute-start.11
  73.4 2.0 collective-permute-start.12
  75.4 1.9 shard_map.131
  77.3 2.6 %collective-permute-start.10 = (bf16[1440,128]{1,0:T(8,128)(2,1)S(1)}, bf16[1440,128]{1,0:T(8,128)(2,1)S(1)}, u32[]{:S(2)}, u32[]{:S(2)}) collective-permute-start(bf16[1440,128]{1,0:T(8,128)(2,1)S(1)} %get-tuple-element.80), channel_id=1, source_target_pairs={{0,48},{16,0},{32,16},{48,32},{64,112},{80,64},{96,80},{112,96},{1... | collective-permute-start | bytes 1105928 | tf_op jit(solution)/shard_map/ppermute | solution.py:45
  79.9 2.7 %collective-permute-start.9 = (bf16[1440,128]{1,0:T(8,128)(2,1)S(1)}, bf16[1440,128]{1,0:T(8,128)(2,1)S(1)}, u32[]{:S(2)}, u32[]{:S(2)}) collective-permute-start(bf16[1440,128]{1,0:T(8,128)(2,1)S(1)} %get-tuple-element.79), channel_id=1, source_target_pairs={{0,48},{16,0},{32,16},{48,32},{64,112},{80,64},{96,80},{112,96},{1... | collective-permute-start | bytes 1105928 | tf_op jit(solution)/shard_map/ppermute | solution.py:45
  82.6 5.7 %collective-permute-done.10.right_b = bf16[1440,128]{1,0:T(8,128)(2,1)S(1)} collective-permute-done((bf16[1440,128]{1,0:T(8,128)(2,1)S(1)}, bf16[1440,128]{1,0:T(8,128)(2,1)S(1)}, u32[]{:S(2)}, u32[]{:S(2)}) %collective-permute-start.10) | collective-permute-done | bytes 368672 | tf_op jit(solution)/shard_map/ppermute | solution.py:45
  88.3 2.9 %collective-permute-done.8.left_a = bf16[1440,128]{1,0:T(8,128)(2,1)S(1)} collective-permute-done((bf16[1440,128]{1,0:T(8,128)(2,1)S(1)}, bf16[1440,128]{1,0:T(8,128)(2,1)S(1)}, u32[]{:S(2)}, u32[]{:S(2)}) %collective-permute-start.8) | collective-permute-done | bytes 368672 | tf_op jit(solution)/shard_map/ppermute | solution.py:41
  91.2 4.4 %collective-permute-done.9.right_a = bf16[1440,128]{1,0:T(8,128)(2,1)S(1)} collective-permute-done((bf16[1440,128]{1,0:T(8,128)(2,1)S(1)}, bf16[1440,128]{1,0:T(8,128)(2,1)S(1)}, u32[]{:S(2)}, u32[]{:S(2)}) %collective-permute-start.9) | collective-permute-done | bytes 368672 | tf_op jit(solution)/shard_map/ppermute | solution.py:45
  95.6 3.8 %collective-permute-start.19 = (bf16[360,2880]{1,0:T(8,128)(2,1)}, bf16[360,2880]{1,0:T(8,128)(2,1)}, u32[]{:S(2)}, u32[]{:S(2)}) collective-permute-start(bf16[360,2880]{1,0:T(8,128)(2,1)} %bitcast.8.refs_5_), channel_id=1, source_target_pairs={{1,17},{3,19},{5,21},{7,23},{9,25},{11,27},{13,29},{15,31},{17,1},... | collective-permute-start | bytes 6220808 | tf_op jit(solution)/shard_map/ppermute | solution.py:477
  99.5 2.1 shard_map.132
  101.6 1.2 copy-done.13
  102.8 1.3 copy-done.11
  104.1 5.4 %all-to-all-start.1 = ((bf16[16,8,2880]{2,1,0:T(8,128)(2,1)}), bf16[16,8,2880]{2,1,0:T(8,128)(2,1)S(1)}, u32[]{:S(2)}, u32[]{:S(2)}) async-start(bf16[16,8,2880]{2,1,0:T(8,128)(2,1)} %bitcast.12), calls=%async_computation.1 | async-start | bytes 1507328 | tf_op jit(solution)/shard_map/all_to_all | solution.py:572
  109.6 2.6 %collective-permute-start.20 = (bf16[360,2880]{1,0:T(8,128)(2,1)S(1)}, bf16[360,2880]{1,0:T(8,128)(2,1)}, u32[]{:S(2)}, u32[]{:S(2)}) collective-permute-start(bf16[360,2880]{1,0:T(8,128)(2,1)S(1)} %bitcast.23), channel_id=1, source_target_pairs={{1,17},{3,19},{5,21},{7,23},{9,25},{11,27},{13,29},{15,31},{17,1},... | collective-permute-start | bytes 6220808 | tf_op jit(solution)/shard_map/ppermute | solution.py:477
  112.2 20.0 %all-to-all-done.1 = bf16[16,8,2880]{2,1,0:T(8,128)(2,1)S(1)} async-done(((bf16[16,8,2880]{2,1,0:T(8,128)(2,1)}), bf16[16,8,2880]{2,1,0:T(8,128)(2,1)S(1)}, u32[]{:S(2)}, u32[]{:S(2)}) %all-to-all-start.1) | async-done | bytes 737312 | tf_op jit(solution)/shard_map/all_to_all | solution.py:572
  132.2 0.1 collective-permute-start.13
  132.3 1.5 collective-permute-start.15
  133.7 1.3 collective-permute-start.17
  135.0 0.2 collective-permute-start.18
  135.2 3.8 %collective-permute-done.13.refs_2_ = bf16[64,2880]{1,0:T(8,128)(2,1)S(1)} collective-permute-done((bf16[64,2880]{1,0:T(8,128)(2,1)S(1)}, bf16[64,2880]{1,0:T(8,128)(2,1)S(1)}, u32[]{:S(2)}, u32[]{:S(2)}) %collective-permute-start.13) | collective-permute-done | bytes 368672 | tf_op jit(solution)/shard_map/ppermute | solution.py:477
  139.0 0.9 collective-permute-start.14
  140.0 1.8 collective-permute-done.15.refs_3_
  141.7 1.6 copy-done.3
  143.3 1.6 copy-done.6
  144.9 1.6 copy-done.9
  146.5 1.6 copy-done.12
  148.1 5.5 %shard_map.133 = (bf16[256,360]{1,0:T(8,128)(2,1)S(1)}, bf16[256,360]{1,0:T(8,128)(2,1)S(1)}) custom-call(bf16[64,2880]{1,0:T(8,128)(2,1)S(1)} %get-tuple-element.122.refs_0_, bf16[64,2880]{1,0:T(8,128)(2,1)S(1)} %get-tuple-element.121.refs_1_, bf16[64,2880]{1,0:T(8,128)(2,1)S(1)} %collective-permute-done.13.refs_2_, ...), custom_call_target="tpu_custom_call" | custom-call | flops 2123366400 | bytes 4194304 | tf_op jit(solution)/shard_map/pallas_call | solution.py:401
  153.6 4.2 %collective-permute-done.16.refs_1_ = bf16[64,2880]{1,0:T(8,128)(2,1)S(1)} collective-permute-done((bf16[64,2880]{1,0:T(8,128)(2,1)S(1)}, bf16[64,2880]{1,0:T(8,128)(2,1)S(1)}, u32[]{:S(2)}, u32[]{:S(2)}) %collective-permute-start.16) | collective-permute-done | bytes 368672 | tf_op jit(solution)/shard_map/ppermute | solution.py:477
  157.9 4.4 %shard_map.134 = (bf16[64,2880]{1,0:T(8,128)(2,1)S(1)}, bf16[64,2880]{1,0:T(8,128)(2,1)S(1)}, bf16[64,2880]{1,0:T(8,128)(2,1)S(1)}, bf16[64,2880]{1,0:T(8,128)(2,1)S(1)}) custom-call(bf16[256,360]{1,0:T(8,128)(2,1)S(1)} %get-tuple-element.97.refs_0_, bf16[256,360]{1,0:T(8,128)(2,1)S(1)} %get-tuple-element.98.refs_1_, bf16[360,2880]{1,0:T(8,128)(2,1)S(1)} %bitcast.24, ...), custom_call_target="tpu_custom_call" | custom-call | flops 1061683200 | bytes 4194304 | tf_op jit(solution)/shard_map/pallas_call | solution.py:401
  162.3 0.1 collective-permute-start.21
  162.4 2.7 %collective-permute-start.22 = (bf16[64,2880]{1,0:T(8,128)(2,1)S(1)}, bf16[64,2880]{1,0:T(8,128)(2,1)S(1)}, u32[]{:S(2)}, u32[]{:S(2)}) collective-permute-start(bf16[64,2880]{1,0:T(8,128)(2,1)S(1)} %get-tuple-element.103), channel_id=1, source_target_pairs={{0,16},{1,49},{2,18},{3,51},{4,20},{5,53},{6,22},{7,55},{8,24},{9,... | collective-permute-start | bytes 1105928 | tf_op jit(solution)/shard_map/ppermute | solution.py:477
  165.1 5.5 %shard_map.135 = (bf16[256,360]{1,0:T(8,128)(2,1)S(1)}, bf16[256,360]{1,0:T(8,128)(2,1)S(1)}) custom-call(bf16[64,2880]{1,0:T(8,128)(2,1)S(1)} %collective-permute-done.14.refs_0_, bf16[64,2880]{1,0:T(8,128)(2,1)S(1)} %collective-permute-done.16.refs_1_, bf16[64,2880]{1,0:T(8,128)(2,1)S(1)} %collective-permute-done.17.refs_2_, ...), custom_call_target="tpu_custom_call" | custom-call | flops 2123366400 | bytes 4194304 | tf_op jit(solution)/shard_map/pallas_call | solution.py:401
  170.6 4.1 %shard_map.136 = (bf16[64,2880]{1,0:T(8,128)(2,1)S(1)}, bf16[64,2880]{1,0:T(8,128)(2,1)S(1)}, bf16[64,2880]{1,0:T(8,128)(2,1)S(1)}, bf16[64,2880]{1,0:T(8,128)(2,1)S(1)}) custom-call(bf16[256,360]{1,0:T(8,128)(2,1)S(1)} %get-tuple-element.108.refs_0_, bf16[256,360]{1,0:T(8,128)(2,1)S(1)} %get-tuple-element.109.refs_1_, bf16[360,2880]{1,0:T(8,128)(2,1)S(1)} %bitcast.25, ...), custom_call_target="tpu_custom_call" | custom-call | flops 1061683200 | bytes 4194304 | tf_op jit(solution)/shard_map/pallas_call | solution.py:401
  174.7 1.1 collective-permute-start.23
  175.8 0.4 collective-permute-start.25
  176.2 5.0 %collective-permute-done.23 = bf16[64,2880]{1,0:T(8,128)(2,1)S(1)} collective-permute-done((bf16[64,2880]{1,0:T(8,128)(2,1)S(1)}, bf16[64,2880]{1,0:T(8,128)(2,1)S(1)}, u32[]{:S(2)}, u32[]{:S(2)}) %collective-permute-start.23) | collective-permute-done | bytes 368672 | tf_op jit(solution)/shard_map/ppermute | solution.py:477
  181.2 0.1 add_convert_fusion.3
  181.3 2.3 %collective-permute-start.24 = (bf16[64,2880]{1,0:T(8,128)(2,1)S(1)}, bf16[64,2880]{1,0:T(8,128)(2,1)S(1)}, u32[]{:S(2)}, u32[]{:S(2)}) collective-permute-start(bf16[64,2880]{1,0:T(8,128)(2,1)S(1)} %add_convert_fusion.3), channel_id=1, source_target_pairs={{0,16},{1,49},{2,18},{3,51},{4,20},{5,53},{6,22},{7,55},{8,24},{9,... | collective-permute-start | bytes 1105928 | tf_op jit(solution)/shard_map/ppermute | solution.py:477
  183.6 0.5 collective-permute-done.25
  184.1 0.1 add_convert_fusion.1
  184.2 0.1 collective-permute-start.26
  184.3 6.7 %collective-permute-done.24 = bf16[64,2880]{1,0:T(8,128)(2,1)S(1)} collective-permute-done((bf16[64,2880]{1,0:T(8,128)(2,1)S(1)}, bf16[64,2880]{1,0:T(8,128)(2,1)S(1)}, u32[]{:S(2)}, u32[]{:S(2)}) %collective-permute-start.24) | collective-permute-done | bytes 368672 | tf_op jit(solution)/shard_map/ppermute | solution.py:477
  191.0 0.1 add_convert_fusion.2
  191.1 0.8 collective-permute-done.26
  191.9 0.1 add_convert_fusion
  192.1 0.1 maximum_bitcast_fusion
  192.1 30.3 %all_to_all.29 = bf16[16,8,2880]{2,1,0:T(8,128)(2,1)S(1)} all-to-all(bf16[16,8,2880]{2,1,0:T(8,128)(2,1)S(1)} %maximum_bitcast_fusion), channel_id=1, replica_groups=mesh['ctx'=8,'exp'=16] {'exp'}, dimensions={0} | all-to-all | bytes 1474560 | tf_op jit(solution)/shard_map/all_to_all | solution.py:577
  222.5 1.6 shard_map.137
  (62 shorter events, 0.2 us)
Async XLA Ops:
  0.0 3.8 %copy-start.21 = (s32[128]{0:T(128)S(1)}, s32[128]{0:T(128)}, u32[]{:S(2)}) copy-start(s32[128]{0:T(128)} %param.18) | copy-start | bytes 1540
  0.0 3.8 %copy-start.15 = (bf16[128,4096]{1,0:T(8,128)(2,1)S(1)}, bf16[128,4096]{1,0:T(8,128)(2,1)}, u32[]{:S(2)}) copy-start(bf16[128,4096]{1,0:T(8,128)(2,1)} %q_ref.1) | copy-start | bytes 3145732
  0.0 3.8 %copy-start.17 = (bf16[128,512]{1,0:T(8,128)(2,1)S(1)}, bf16[128,512]{1,0:T(8,128)(2,1)}, u32[]{:S(2)}) copy-start(bf16[128,512]{1,0:T(8,128)(2,1)} %k_ref.1) | copy-start | bytes 393220
  0.0 3.8 %copy-start.18 = (bf16[128,512]{1,0:T(8,128)(2,1)S(1)}, bf16[128,512]{1,0:T(8,128)(2,1)}, u32[]{:S(2)}) copy-start(bf16[128,512]{1,0:T(8,128)(2,1)} %v_ref.1) | copy-start | bytes 393220
  1.6 23.4 %collective-permute-start = (bf16[1440,512]{1,0:T(8,128)(2,1)S(1)}, bf16[1440,512]{1,0:T(8,128)(2,1)S(1)}, u32[]{:S(2)}, u32[]{:S(2)}) collective-permute-start(bf16[1440,512]{1,0:T(8,128)(2,1)S(1)} %dynamic-slice_bitcast_fusion), channel_id=1, source_target_pairs={{0,66},{1,65},{2,64},{3,67},{4,70},{5,69},{6,68},{7,71},{8,74},{9,... | collective-permute-start | bytes 4423688 | tf_op jit(solution)/shard_map/ppermute | solution.py:477
  4.0 27.3 %copy-start.2 = (bf16[1,2880,360]{1,2,0:T(8,128)(2,1)S(1)}, bf16[1,2880,360]{1,2,0:T(8,128)(2,1)}, u32[]{:S(2)}) copy-start(bf16[1,2880,360]{1,2,0:T(8,128)(2,1)} %param.21) | copy-start | bytes 6220804
  4.1 38.9 %copy-start.22 = (f32[64]{0:T(128)S(1)}, f32[64]{0:T(128)}, u32[]{:S(2)}) copy-start(f32[64]{0:T(128)} %sinks.3) | copy-start | bytes 772
  25.1 23.7 %copy-start = (bf16[512,2880]{0,1:T(8,128)(2,1)S(1)}, bf16[512,2880]{0,1:T(8,128)(2,1)}, u32[]{:S(2)}) copy-start(bf16[512,2880]{0,1:T(8,128)(2,1)} %param.20) | copy-start | bytes 8847364
  25.1 11.7 %collective-permute-start.1 = (bf16[4,144,256]{2,1,0:T(8,128)(2,1)S(1)}, bf16[4,144,256]{2,1,0:T(8,128)(2,1)S(1)}, u32[]{:S(2)}, u32[]{:S(2)}) collective-permute-start(bf16[4,144,256]{2,1,0:T(8,128)(2,1)S(1)} %slice.9), channel_id=1, source_target_pairs={{0,64},{16,80},{32,96},{48,112},{1,65},{17,81},{33,97},{49,113},{2... | collective-permute-start | bytes 884744 | tf_op jit(solution)/shard_map/ppermute | solution.py:543
  31.3 41.2 %collective-permute-start.7 = (bf16[360,2880]{1,0:T(8,128)(2,1)S(1)}, bf16[360,2880]{1,0:T(8,128)(2,1)S(1)}, u32[]{:S(2)}, u32[]{:S(2)}) collective-permute-start(bf16[360,2880]{1,0:T(8,128)(2,1)S(1)} %bitcast.26), channel_id=1, source_target_pairs={{1,17},{3,19},{5,21},{7,23},{9,25},{11,27},{13,29},{15,31},{17,1},... | collective-permute-start | bytes 6220808 | tf_op jit(solution)/shard_map/ppermute | solution.py:477
  36.7 35.8 %collective-permute-start.6 = (bf16[360,2880]{1,0:T(8,128)(2,1)S(1)}, bf16[360,2880]{1,0:T(8,128)(2,1)S(1)}, u32[]{:S(2)}, u32[]{:S(2)}) collective-permute-start(bf16[360,2880]{1,0:T(8,128)(2,1)S(1)} %bitcast.27), channel_id=1, source_target_pairs={{0,64},{2,66},{4,68},{6,70},{8,72},{10,74},{12,76},{14,78},{16,80}... | collective-permute-start | bytes 6220808 | tf_op jit(solution)/shard_map/ppermute | solution.py:477
  37.5 11.3 %collective-permute-start.2 = (bf16[1440,512]{1,0:T(8,128)(2,1)S(1)}, bf16[1440,512]{1,0:T(8,128)(2,1)S(1)}, u32[]{:S(2)}, u32[]{:S(2)}) collective-permute-start(bf16[1440,512]{1,0:T(8,128)(2,1)S(1)} %collective-permute-done.w_first), channel_id=1, source_target_pairs={{0,1},{1,0},{2,3},{3,2},{4,5},{5,4},{6,7},{7,6},{8,9},{9,8},{10,11... | collective-permute-start | bytes 4423688 | tf_op jit(solution)/shard_map/ppermute | solution.py:477
  50.6 18.0 %collective-permute-start.3 = (bf16[1440,128]{1,0:T(8,128)(2,1)S(1)}, bf16[1440,128]{1,0:T(8,128)(2,1)S(1)}, u32[]{:S(2)}, u32[]{:S(2)}) collective-permute-start(bf16[1440,128]{1,0:T(8,128)(2,1)S(1)} %get-tuple-element.66), channel_id=1, source_target_pairs={{0,16},{16,32},{32,48},{48,0},{64,80},{80,96},{96,112},{112,64},{1... | collective-permute-start | bytes 1105928 | tf_op jit(solution)/shard_map/ppermute | solution.py:41
  51.4 17.2 %collective-permute-start.4 = (bf16[1440,128]{1,0:T(8,128)(2,1)S(1)}, bf16[1440,128]{1,0:T(8,128)(2,1)S(1)}, u32[]{:S(2)}, u32[]{:S(2)}) collective-permute-start(bf16[1440,128]{1,0:T(8,128)(2,1)S(1)} %get-tuple-element.67), channel_id=1, source_target_pairs={{0,48},{16,0},{32,16},{48,32},{64,112},{80,64},{96,80},{112,96},{1... | collective-permute-start | bytes 1105928 | tf_op jit(solution)/shard_map/ppermute | solution.py:45
  53.3 20.0 %copy-start.1 = (bf16[1,360,2880]{2,1,0:T(8,128)(2,1)S(1)}, bf16[1,360,2880]{2,1,0:T(8,128)(2,1)}, u32[]{:S(2)}) copy-start(bf16[1,360,2880]{2,1,0:T(8,128)(2,1)} %param.23) | copy-start | bytes 6220804
  53.3 19.2 %collective-permute-start.5 = (bf16[1440,128]{1,0:T(8,128)(2,1)S(1)}, bf16[1440,128]{1,0:T(8,128)(2,1)S(1)}, u32[]{:S(2)}, u32[]{:S(2)}) collective-permute-start(bf16[1440,128]{1,0:T(8,128)(2,1)S(1)} %get-tuple-element.68), channel_id=1, source_target_pairs={{0,16},{16,32},{32,48},{48,0},{64,80},{80,96},{96,112},{112,64},{1... | collective-permute-start | bytes 1105928 | tf_op jit(solution)/shard_map/ppermute | solution.py:41
  72.5 4.8 %copy-start.5 = (bf16[360,2880]{1,0:T(8,128)(2,1)}, bf16[360,2880]{1,0:T(8,128)(2,1)S(1)}, u32[]{:S(2)}) copy-start(bf16[360,2880]{1,0:T(8,128)(2,1)S(1)} %collective-permute-done.7.refs_7_) | copy-start | bytes 6220804
  72.5 4.8 %copy-start.8 = (bf16[360,2880]{1,0:T(8,128)(2,1)}, bf16[360,2880]{1,0:T(8,128)(2,1)S(1)}, u32[]{:S(2)}) copy-start(bf16[360,2880]{1,0:T(8,128)(2,1)S(1)} %collective-permute-done.6.refs_6_) | copy-start | bytes 6220804
  72.5 30.3 %collective-permute-start.11 = (bf16[360,2880]{1,0:T(8,128)(2,1)}, bf16[360,2880]{1,0:T(8,128)(2,1)S(1)}, u32[]{:S(2)}, u32[]{:S(2)}) collective-permute-start(bf16[360,2880]{1,0:T(8,128)(2,1)} %bitcast.8.refs_5_), channel_id=1, source_target_pairs={{0,64},{2,66},{4,68},{6,70},{8,72},{10,74},{12,76},{14,78},{16,80}... | collective-permute-start | bytes 6220808 | tf_op jit(solution)/shard_map/ppermute | solution.py:477
  73.4 38.8 %collective-permute-start.12 = (bf16[360,2880]{1,0:T(8,128)(2,1)S(1)}, bf16[360,2880]{1,0:T(8,128)(2,1)}, u32[]{:S(2)}, u32[]{:S(2)}) collective-permute-start(bf16[360,2880]{1,0:T(8,128)(2,1)S(1)} %bitcast.22), channel_id=1, source_target_pairs={{0,64},{2,66},{4,68},{6,70},{8,72},{10,74},{12,76},{14,78},{16,80}... | collective-permute-start | bytes 6220808 | tf_op jit(solution)/shard_map/ppermute | solution.py:477
  75.4 24.1 %copy-start.23 = (f32[2880]{0:T(1024)S(1)}, f32[2880]{0:T(1024)}, u32[]{:S(2)}) copy-start(f32[2880]{0:T(1024)} %param.19) | copy-start | bytes 34564
  75.4 24.1 %copy-start.16 = (bf16[128,2880]{0,1:T(8,128)(2,1)S(1)}, bf16[128,2880]{0,1:T(8,128)(2,1)}, u32[]{:S(2)}) copy-start(bf16[128,2880]{0,1:T(8,128)(2,1)} %param.13) | copy-start | bytes 2211844
  75.4 24.1 %copy-start.19 = (s32[128,4]{0,1:T(4,128)S(1)}, s32[128,4]{0,1:T(4,128)}, u32[]{:S(2)}) copy-start(s32[128,4]{0,1:T(4,128)} %param.24) | copy-start | bytes 6148
  77.3 10.9 %collective-permute-start.10 = (bf16[1440,128]{1,0:T(8,128)(2,1)S(1)}, bf16[1440,128]{1,0:T(8,128)(2,1)S(1)}, u32[]{:S(2)}, u32[]{:S(2)}) collective-permute-start(bf16[1440,128]{1,0:T(8,128)(2,1)S(1)} %get-tuple-element.80), channel_id=1, source_target_pairs={{0,48},{16,0},{32,16},{48,32},{64,112},{80,64},{96,80},{112,96},{1... | collective-permute-start | bytes 1105928 | tf_op jit(solution)/shard_map/ppermute | solution.py:45
  79.9 11.2 %collective-permute-start.8 = (bf16[1440,128]{1,0:T(8,128)(2,1)S(1)}, bf16[1440,128]{1,0:T(8,128)(2,1)S(1)}, u32[]{:S(2)}, u32[]{:S(2)}) collective-permute-start(bf16[1440,128]{1,0:T(8,128)(2,1)S(1)} %get-tuple-element.77), channel_id=1, source_target_pairs={{0,16},{16,32},{32,48},{48,0},{64,80},{80,96},{96,112},{112,64},{1... | collective-permute-start | bytes 1105928 | tf_op jit(solution)/shard_map/ppermute | solution.py:41
  79.9 15.7 %collective-permute-start.9 = (bf16[1440,128]{1,0:T(8,128)(2,1)S(1)}, bf16[1440,128]{1,0:T(8,128)(2,1)S(1)}, u32[]{:S(2)}, u32[]{:S(2)}) collective-permute-start(bf16[1440,128]{1,0:T(8,128)(2,1)S(1)} %get-tuple-element.79), channel_id=1, source_target_pairs={{0,48},{16,0},{32,16},{48,32},{64,112},{80,64},{96,80},{112,96},{1... | collective-permute-start | bytes 1105928 | tf_op jit(solution)/shard_map/ppermute | solution.py:45
  95.6 39.4 %collective-permute-start.19 = (bf16[360,2880]{1,0:T(8,128)(2,1)}, bf16[360,2880]{1,0:T(8,128)(2,1)}, u32[]{:S(2)}, u32[]{:S(2)}) collective-permute-start(bf16[360,2880]{1,0:T(8,128)(2,1)} %bitcast.8.refs_5_), channel_id=1, source_target_pairs={{1,17},{3,19},{5,21},{7,23},{9,25},{11,27},{13,29},{15,31},{17,1},... | collective-permute-start | bytes 6220808 | tf_op jit(solution)/shard_map/ppermute | solution.py:477
  101.6 1.2 copy-start.13
  102.8 1.3 copy-start.11
  104.1 28.0 %all-to-all-start.1 = ((bf16[16,8,2880]{2,1,0:T(8,128)(2,1)}), bf16[16,8,2880]{2,1,0:T(8,128)(2,1)S(1)}, u32[]{:S(2)}, u32[]{:S(2)}) async-start(bf16[16,8,2880]{2,1,0:T(8,128)(2,1)} %bitcast.12), calls=%async_computation.1 | async-start | bytes 1507328 | tf_op jit(solution)/shard_map/all_to_all | solution.py:572
  109.6 48.3 %collective-permute-start.20 = (bf16[360,2880]{1,0:T(8,128)(2,1)S(1)}, bf16[360,2880]{1,0:T(8,128)(2,1)}, u32[]{:S(2)}, u32[]{:S(2)}) collective-permute-start(bf16[360,2880]{1,0:T(8,128)(2,1)S(1)} %bitcast.23), channel_id=1, source_target_pairs={{1,17},{3,19},{5,21},{7,23},{9,25},{11,27},{13,29},{15,31},{17,1},... | collective-permute-start | bytes 6220808 | tf_op jit(solution)/shard_map/ppermute | solution.py:477
  132.2 6.8 %collective-permute-start.13 = (bf16[64,2880]{1,0:T(8,128)(2,1)S(1)}, bf16[64,2880]{1,0:T(8,128)(2,1)S(1)}, u32[]{:S(2)}, u32[]{:S(2)}) collective-permute-start(bf16[64,2880]{1,0:T(8,128)(2,1)S(1)} %get-tuple-element.122.refs_0_), channel_id=1, source_target_pairs={{0,16},{1,49},{2,18},{3,51},{4,20},{5,53},{6,22},{7,55},{8,24},{9,... | collective-permute-start | bytes 1105928 | tf_op jit(solution)/shard_map/ppermute | solution.py:477
  132.3 9.4 %collective-permute-start.15 = (bf16[64,2880]{1,0:T(8,128)(2,1)S(1)}, bf16[64,2880]{1,0:T(8,128)(2,1)S(1)}, u32[]{:S(2)}, u32[]{:S(2)}) collective-permute-start(bf16[64,2880]{1,0:T(8,128)(2,1)S(1)} %get-tuple-element.121.refs_1_), channel_id=1, source_target_pairs={{16,0},{49,1},{18,2},{51,3},{20,4},{53,5},{22,6},{55,7},{24,8},{57... | collective-permute-start | bytes 1105928 | tf_op jit(solution)/shard_map/ppermute | solution.py:477
  133.7 19.9 %collective-permute-start.17 = (bf16[64,2880]{1,0:T(8,128)(2,1)S(1)}, bf16[64,2880]{1,0:T(8,128)(2,1)S(1)}, u32[]{:S(2)}, u32[]{:S(2)}) collective-permute-start(bf16[64,2880]{1,0:T(8,128)(2,1)S(1)} %get-tuple-element.121.refs_1_), channel_id=1, source_target_pairs={{0,16},{1,49},{2,18},{3,51},{4,20},{5,53},{6,22},{7,55},{8,24},{9,... | collective-permute-start | bytes 1105928 | tf_op jit(solution)/shard_map/ppermute | solution.py:477
  135.0 18.6 %collective-permute-start.18 = (bf16[64,2880]{1,0:T(8,128)(2,1)S(1)}, bf16[64,2880]{1,0:T(8,128)(2,1)S(1)}, u32[]{:S(2)}, u32[]{:S(2)}) collective-permute-start(bf16[64,2880]{1,0:T(8,128)(2,1)S(1)} %get-tuple-element.122.refs_0_), channel_id=1, source_target_pairs={{16,0},{49,1},{18,2},{51,3},{20,4},{53,5},{22,6},{55,7},{24,8},{57... | collective-permute-start | bytes 1105928 | tf_op jit(solution)/shard_map/ppermute | solution.py:477
  139.0 14.6 %collective-permute-start.14 = (bf16[64,2880]{1,0:T(8,128)(2,1)S(1)}, bf16[64,2880]{1,0:T(8,128)(2,1)S(1)}, u32[]{:S(2)}, u32[]{:S(2)}) collective-permute-start(bf16[64,2880]{1,0:T(8,128)(2,1)S(1)} %collective-permute-done.13.refs_2_), channel_id=1, source_target_pairs={{0,16},{1,49},{2,18},{3,51},{4,20},{5,53},{6,22},{7,55},{8,24},{9,... | collective-permute-start | bytes 1105928 | tf_op jit(solution)/shard_map/ppermute | solution.py:477
  141.7 16.2 %collective-permute-start.16 = (bf16[64,2880]{1,0:T(8,128)(2,1)S(1)}, bf16[64,2880]{1,0:T(8,128)(2,1)S(1)}, u32[]{:S(2)}, u32[]{:S(2)}) collective-permute-start(bf16[64,2880]{1,0:T(8,128)(2,1)S(1)} %collective-permute-done.15.refs_3_), channel_id=1, source_target_pairs={{16,0},{49,1},{18,2},{51,3},{20,4},{53,5},{22,6},{55,7},{24,8},{57... | collective-permute-start | bytes 1105928 | tf_op jit(solution)/shard_map/ppermute | solution.py:477
  141.7 1.6 copy-start.3
  143.3 1.6 copy-start.6
  144.9 1.6 copy-start.9
  146.5 1.6 copy-start.12
  157.9 7.2 %copy-start.4 = (bf16[1,2880,360]{1,2,0:T(8,128)(2,1)S(1)}, bf16[1,2880,360]{1,2,0:T(8,128)(2,1)}, u32[]{:S(2)}) copy-start(bf16[1,2880,360]{1,2,0:T(8,128)(2,1)} %param.21) | copy-start | bytes 6220804
  157.9 7.2 %copy-start.7 = (bf16[360,2880]{1,0:T(8,128)(2,1)S(1)}, bf16[360,2880]{1,0:T(8,128)(2,1)}, u32[]{:S(2)}) copy-start(bf16[360,2880]{1,0:T(8,128)(2,1)} %copy-done.5) | copy-start | bytes 6220804
  157.9 7.2 %copy-start.10 = (bf16[360,2880]{1,0:T(8,128)(2,1)S(1)}, bf16[360,2880]{1,0:T(8,128)(2,1)}, u32[]{:S(2)}) copy-start(bf16[360,2880]{1,0:T(8,128)(2,1)} %copy-done.8) | copy-start | bytes 6220804
  162.3 12.4 %collective-permute-start.21 = (bf16[64,2880]{1,0:T(8,128)(2,1)S(1)}, bf16[64,2880]{1,0:T(8,128)(2,1)S(1)}, u32[]{:S(2)}, u32[]{:S(2)}) collective-permute-start(bf16[64,2880]{1,0:T(8,128)(2,1)S(1)} %get-tuple-element.102), channel_id=1, source_target_pairs={{16,0},{49,1},{18,2},{51,3},{20,4},{53,5},{22,6},{55,7},{24,8},{57... | collective-permute-start | bytes 1105928 | tf_op jit(solution)/shard_map/ppermute | solution.py:477
  162.4 12.3 %collective-permute-start.22 = (bf16[64,2880]{1,0:T(8,128)(2,1)S(1)}, bf16[64,2880]{1,0:T(8,128)(2,1)S(1)}, u32[]{:S(2)}, u32[]{:S(2)}) collective-permute-start(bf16[64,2880]{1,0:T(8,128)(2,1)S(1)} %get-tuple-element.103), channel_id=1, source_target_pairs={{0,16},{1,49},{2,18},{3,51},{4,20},{5,53},{6,22},{7,55},{8,24},{9,... | collective-permute-start | bytes 1105928 | tf_op jit(solution)/shard_map/ppermute | solution.py:477
  174.7 6.5 %collective-permute-start.23 = (bf16[64,2880]{1,0:T(8,128)(2,1)S(1)}, bf16[64,2880]{1,0:T(8,128)(2,1)S(1)}, u32[]{:S(2)}, u32[]{:S(2)}) collective-permute-start(bf16[64,2880]{1,0:T(8,128)(2,1)S(1)} %get-tuple-element.116), channel_id=1, source_target_pairs={{0,16},{1,49},{2,18},{3,51},{4,20},{5,53},{6,22},{7,55},{8,24},{9,... | collective-permute-start | bytes 1105928 | tf_op jit(solution)/shard_map/ppermute | solution.py:477
  175.8 8.3 %collective-permute-start.25 = (bf16[64,2880]{1,0:T(8,128)(2,1)S(1)}, bf16[64,2880]{1,0:T(8,128)(2,1)S(1)}, u32[]{:S(2)}, u32[]{:S(2)}) collective-permute-start(bf16[64,2880]{1,0:T(8,128)(2,1)S(1)} %get-tuple-element.120), channel_id=1, source_target_pairs={{16,0},{49,1},{18,2},{51,3},{20,4},{53,5},{22,6},{55,7},{24,8},{57... | collective-permute-start | bytes 1105928 | tf_op jit(solution)/shard_map/ppermute | solution.py:477
  181.3 9.7 %collective-permute-start.24 = (bf16[64,2880]{1,0:T(8,128)(2,1)S(1)}, bf16[64,2880]{1,0:T(8,128)(2,1)S(1)}, u32[]{:S(2)}, u32[]{:S(2)}) collective-permute-start(bf16[64,2880]{1,0:T(8,128)(2,1)S(1)} %add_convert_fusion.3), channel_id=1, source_target_pairs={{0,16},{1,49},{2,18},{3,51},{4,20},{5,53},{6,22},{7,55},{8,24},{9,... | collective-permute-start | bytes 1105928 | tf_op jit(solution)/shard_map/ppermute | solution.py:477
  184.2 7.7 %collective-permute-start.26 = (bf16[64,2880]{1,0:T(8,128)(2,1)S(1)}, bf16[64,2880]{1,0:T(8,128)(2,1)S(1)}, u32[]{:S(2)}, u32[]{:S(2)}) collective-permute-start(bf16[64,2880]{1,0:T(8,128)(2,1)S(1)} %add_convert_fusion.1), channel_id=1, source_target_pairs={{16,0},{49,1},{18,2},{51,3},{20,4},{53,5},{22,6},{55,7},{24,8},{57... | collective-permute-start | bytes 1105928 | tf_op jit(solution)/shard_map/ppermute | solution.py:477
  191.9 30.6 %copy-start.14 = (f32[2880,128]{1,0:T(8,128)S(1)}, f32[2880,128]{1,0:T(8,128)}, u32[]{:S(2)}) copy-start(f32[2880,128]{1,0:T(8,128)} %copy-done.13) | copy-start | bytes 4423684
  191.9 30.6 %copy-start.20 = (f32[128,4]{0,1:T(4,128)S(1)}, f32[128,4]{0,1:T(4,128)}, u32[]{:S(2)}) copy-start(f32[128,4]{0,1:T(4,128)} %param.25) | copy-start | bytes 6148
